TPU v7x, 32 devices: a whole 2x2x4 slice. The times are simulated.
32 devices in a mesh: group: 2 (over y), replica: 4 (over z), tensor: 4 (over x, core).
Axes of the slice: x: 2, y: 2, z: 4, core: 2. Of those that a mesh axis runs over, the one named last changes fastest.
Arguments:
- suffix_hidden: bfloat16 [2048, 8192], P(('group', 'replica'), 'tensor'), parts along dimension 0, may hold values from -6 to 6
- base_query: bfloat16 [2048, 8192], P(('group', 'replica'), 'tensor'), parts along dimension 0
- suffix_key_value: bfloat16 [2048, 8, 256], P(('group', 'replica'), 'tensor'), parts along dimension 0, may hold values from -6 to 6
- tenant_prefix_cache: bfloat16 [8, 1024, 8, 256], P(('group', 'replica'), None, 'tensor'), parts along dimension 0
- adapter_down: bfloat16 [2, 32, 8192], P(None, None, 'tensor'), may hold values from -0.0625 to 0.0625
- adapter_up_query: bfloat16 [2, 16, 8192], P(None, None, 'tensor'), may hold values from -1.5 to 1.5
- adapter_up_value: bfloat16 [2, 16, 8, 128], P(None, None, 'tensor'), may hold values from -1.5 to 1.5
- tenant_replica: int32 [8], P('group'), parts along dimension 0, may hold values from 0 to 3, as said below
- tenant_of_request: int32 [8], P(('group', 'replica')), parts along dimension 0, may hold values from 0 to 3, as said below
- suffix_blocks: int32 [8], P(('group', 'replica')), parts along dimension 0, may hold values from 1 to 2, as said below
- request_adapter: int32 [8], P(('group', 'replica')), parts along dimension 0, may hold values from 0 to 1
Outputs:
- attended: bfloat16 [2048, 8192], P(('group', 'replica'), 'tensor'), parts along dimension 0
There are 2 independent parts, one for each index of `group`. A program takes and returns all parts, laid end to end along the dimension named above; an argument that names none is the same for every part. Nothing has to cross between parts.
Inputs may be any that keep to these rules, and one draw needn't show every extreme that they name: `tenant_replica`: each replica owns exactly one tenant. `tenant_of_request`: the owner of a replica's tenant lies 0 to 3 replicas before it in cycle order (owner = index minus distance, modulo 4); some replica reads at distance 4 - 1. `suffix_blocks`: some replica's request has 2 blocks.
All inputs are finite; a program needn't handle non-finite values.
Results may differ from a plain program's by a relative error of at most 0.012.
Values may be sent and summed in bfloat16 or wider, within the bound.
No kernel may reach another device: no remote copies, remote signals or barrier semaphores. Data moves between devices by JAX's collectives and lax.ppermute only.
A program may use at most 64 MiB of HBM per device.

v0:
```python
import math

import jax
import jax.numpy as jnp
from jax import lax
from jax.sharding import PartitionSpec as P

STRETCH = 128
READ_SPAN = 4


def passed_along(shard, axis, by):
    size = lax.axis_size(axis)
    return lax.ppermute(shard, axis, [(i, (i + by) % size) for i in range(size)])


def attend(query, all_keys, values, prefix_len):
    row_count = query.shape[0]
    scores = jnp.einsum(
        "rgd,kd->grk", query, all_keys, preferred_element_type=jnp.float32
    ) / math.sqrt(query.shape[-1])
    key_index = jnp.arange(all_keys.shape[0])
    row_index = jnp.arange(row_count)
    allowed = (key_index[None, :] < prefix_len) | (
        key_index[None, :] - prefix_len <= row_index[:, None]
    )
    scores = jnp.where(allowed[None], scores, -jnp.inf)
    largest = jnp.max(scores, axis=2, keepdims=True)
    powers = jnp.exp(scores - largest)
    weights = (powers / jnp.sum(powers, axis=2, keepdims=True)).astype(jnp.bfloat16)
    return jnp.einsum("grk,kd->rgd", weights, values, preferred_element_type=jnp.float32).astype(
        jnp.bfloat16
    )


def on_device(
    suffix_hidden,
    base_query,
    suffix_key_value,
    tenant_prefix_cache,
    adapter_down,
    adapter_up_query,
    adapter_up_value,
    tenant_replica,
    tenant_of_request,
    suffix_blocks,
    request_adapter,
):
    row_count = suffix_hidden.shape[0]
    head_width = suffix_key_value.shape[2] // 2
    local_key_value = suffix_key_value.shape[1]
    local_query = base_query.shape[1] // head_width
    adapter_rank_size = adapter_down.shape[1] // 2
    adapter_choice = request_adapter[0]
    own_page = tenant_prefix_cache[0]
    position = lax.axis_index("replica")
    replicas = lax.axis_size("replica")
    owner_slot = tenant_replica[tenant_of_request[0]]
    distance = jnp.remainder(position - owner_slot, replicas)
    chosen = own_page
    for offset in range(1, READ_SPAN):
        moved = passed_along(own_page, "replica", offset)
        chosen = jnp.where(distance == offset, moved, chosen)
    down_matrix_rows = lax.dynamic_index_in_dim(adapter_down, adapter_choice, 0, keepdims=False)
    partial_low = lax.dot_general(
        suffix_hidden,
        down_matrix_rows,
        (((1,), (1,)), ((), ())),
        preferred_element_type=jnp.float32,
    )
    rank_projection = lax.psum(partial_low, "tensor").astype(jnp.bfloat16)
    query_up_matrix = lax.dynamic_index_in_dim(adapter_up_query, adapter_choice, 0, keepdims=False)
    query_update = jnp.dot(
        rank_projection[:, :adapter_rank_size], query_up_matrix, preferred_element_type=jnp.float32
    )
    query = (base_query.astype(jnp.float32) + query_update).astype(jnp.bfloat16)
    value_up_matrix = lax.dynamic_index_in_dim(
        adapter_up_value, adapter_choice, 0, keepdims=False
    ).reshape(adapter_rank_size, local_key_value * head_width)
    value_delta = jnp.dot(
        rank_projection[:, adapter_rank_size:], value_up_matrix, preferred_element_type=jnp.float32
    ).reshape(row_count, local_key_value, head_width)
    suffix_value = (suffix_key_value[..., head_width:].astype(jnp.float32) + value_delta).astype(
        jnp.bfloat16
    )
    prefix_len = chosen.shape[0]
    all_keys = jnp.concatenate(
        [chosen[..., :head_width], suffix_key_value[..., :head_width]], axis=0
    )
    values = jnp.concatenate([chosen[..., head_width:], suffix_value], axis=0)
    grouped = query.reshape(row_count, local_key_value, local_query // local_key_value, head_width)
    per_head = [
        attend(grouped[:, head], all_keys[:, head], values[:, head], prefix_len)
        for head in range(local_key_value)
    ]
    result = jnp.stack(per_head, axis=1).reshape(row_count, local_query * head_width)
    live_rows = jnp.arange(row_count) < suffix_blocks[0] * STRETCH
    return jnp.where(live_rows[:, None], result, jnp.zeros_like(result))


def solution(mesh):
    in_specs = (
        P(("group", "replica"), "tensor"),
        P(("group", "replica"), "tensor"),
        P(("group", "replica"), "tensor", None),
        P(("group", "replica"), None, "tensor", None),
        P(None, None, "tensor"),
        P(None, None, "tensor"),
        P(None, None, "tensor", None),
        P("group"),
        P(("group", "replica")),
        P(("group", "replica")),
        P(("group", "replica")),
    )
    out_specs = P(("group", "replica"), "tensor")
    return jax.shard_map(
        on_device, mesh=mesh, in_specs=in_specs, out_specs=out_specs, check_vma=False
    )
```

profile of v0, /device:TPU:0, one launch (start us, length us, event | category | flops | bytes accessed | tf_op | source)
XLA Modules:
  0.0 122.6 jit_solution(9840852019301958957)
XLA Ops:
  0.0 1.5 %copy.81 = bf16[1,1024,2,256]{3,1,2,0:T(8,128)(2,1)S(1)} copy(bf16[1,1024,2,256]{3,2,1,0:T(2,128)(2,1)} %param.14) | data formatting | bytes 2097152 | tf_op args[3]
  1.5 5.1 %collective-permute-start = (bf16[1024,2,256]{2,0,1:T(8,128)(2,1)S(1)}, bf16[1024,2,256]{2,0,1:T(8,128)(2,1)}, u32[]{:S(2)}, u32[]{:S(2)}) collective-permute-start(bf16[1024,2,256]{2,0,1:T(8,128)(2,1)S(1)} %bitcast.136), channel_id=1, source_target_pairs={{0,12},{4,0},{8,4},{12,8},{1,13},{5,1},{9,5},{13,9},{2,14},{6,2},{... | collective-permute-start | bytes 3145736 | tf_op jit(solution)/shard_map/ppermute | solution.py:14
  6.6 1.0 collective-permute-start.2
  8.3 0.6 dynamic_slice.15
  10.2 0.4 convolution_bitcast_fusion
  10.6 11.1 %psum.7 = bf16[256,32]{0,1:T(8,128)(2,1)S(1)} all-reduce(f32[256,32]{0,1:T(8,128)S(1)} %convolution_bitcast_fusion), channel_id=1, replica_groups=mesh['group'=2,'replica'=4,'tensor'=4] {'tensor'}, use_global_device_ids=true, to_apply=%region_0.1 | all-reduce | flops 8192 | bytes 49152 | tf_op jit(solution)/shard_map/psum | solution.py:71
  21.7 1.3 %fusion.17 = bf16[32,8,16,128]{3,1,2,0:T(8,128)(2,1)S(1)} fusion(bf16[256,2048]{1,0:T(8,128)(2,1)S(1)} %copy-done.2, bf16[2,16,2048]{2,1,0:T(8,128)(2,1)} %param.16, s32[]{:T(128)S(6)} %select_n.57, bf16[256,32]{0,1:T(8,128)(2,1)S(1)} %psum.7), kind=kOutput, calls=%fused_computation.22 | convolution fusion | flops 18350080 | bytes 2170884 | tf_op jit(solution)/shard_map/dot_general | solution.py:73
  23.1 0.2 copy.45
  23.3 0.7 copy-done.4
  24.0 0.2 fusion.72
  24.2 0.7 copy.40
  25.5 0.9 fusion.23
  26.5 1.1 fusion.18
  27.6 2.6 %collective-permute-done = bf16[1024,2,256]{2,0,1:T(8,128)(2,1)} collective-permute-done((bf16[1024,2,256]{2,0,1:T(8,128)(2,1)S(1)}, bf16[1024,2,256]{2,0,1:T(8,128)(2,1)}, u32[]{:S(2)}, u32[]{:S(2)}) %collective-permute-start) | collective-permute-done | bytes 1048608 | tf_op jit(solution)/shard_map/ppermute | solution.py:14
  30.2 66.2 %collective-permute-done.1 = bf16[1024,2,256]{2,0,1:T(8,128)(2,1)} collective-permute-done((bf16[1024,2,256]{2,0,1:T(8,128)(2,1)S(1)}, bf16[1024,2,256]{2,0,1:T(8,128)(2,1)}, u32[]{:S(2)}, u32[]{:S(2)}) %collective-permute-start.1) | collective-permute-done | bytes 1048608 | tf_op jit(solution)/shard_map/ppermute | solution.py:14
  96.4 1.6 %select_select_fusion = bf16[1024,2,256]{2,0,1:T(8,128)(2,1)S(1)} fusion(bf16[1024,2,256]{2,0,1:T(8,128)(2,1)} %collective-permute-done, bf16[1024,2,256]{2,0,1:T(8,128)(2,1)} %collective-permute-done.1, bf16[1024,2,256]{2,0,1:T(8,128)(2,1)} %collective-permute-done.2, pred[]{:T(512)S(6)} %eq.13, pred[]{:T(512)S(6)} %eq.12, pred[]{:T(512)S(6)} %eq.11, ...), kind=kLoop, calls=%fused_computation.34 | loop fusion | flops 1572864 | bytes 5242883 | tf_op jit(solution)/shard_map/jit(_where)/select_n | solution.py:63
  98.0 0.2 fusion.71
  98.2 4.2 %fusion.76 = f32[8,256]{1,0:T(8,128)S(1)} fusion(pred[256,1280]{0,1:T(8,128)(4,1)S(1)} %fusion.18, bf16[256,1,8,128]{3,2,1,0:T(8,128)(2,1)S(1)} %get-tuple-element.5, bf16[1024,2,128]{2,0,1:T(8,128)(2,1)S(1)} %get-tuple-element.8, bf16[256,2,128]{2,0,1:T(8,128)(2,1)} %copy.40), kind=kOutput, calls=%fused_computation.82 | convolution fusion | flops 682231040 | bytes 1515520 | tf_op jit(solution)/shard_map/sub | solution.py:29
  102.4 4.2 %fusion.73 = f32[8,256]{1,0:T(8,128)S(1)} fusion(pred[256,1280]{0,1:T(8,128)(4,1)S(1)} %fusion.18, bf16[256,1,8,128]{3,2,1,0:T(8,128)(2,1)S(1)} %get-tuple-element.6, bf16[256,2,128]{2,0,1:T(8,128)(2,1)} %copy.40, bf16[1024,2,128]{2,0,1:T(8,128)(2,1)S(1)} %get-tuple-element.8), kind=kOutput, calls=%fused_computation.81 | convolution fusion | flops 682231040 | bytes 1515520 | tf_op jit(solution)/shard_map/sub | solution.py:29
  106.6 6.4 %fusion.21 = bf16[256,1,8,128]{0,3,2,1:T(8,128)(2,1)} fusion(f32[8,256]{1,0:T(8,128)S(1)} %fusion.76, bf16[1024,2,128]{2,0,1:T(8,128)(2,1)S(1)} %get-tuple-element.7, bf16[256,2,128]{2,0,1:T(8,128)(2,1)} %fusion.23, pred[256,1280]{0,1:T(8,128)(4,1)S(1)} %fusion.18, bf16[256,1,8,128]{3,2,1,0:T(8,128)(2,1)S(1)} %get-tuple-element.5, ...), kind=kOutput, calls=%fused_computation.27 | convolution fusion | flops 1356860672 | bytes 2695168 | tf_op jit(solution)/shard_map/grk,kd->rgd/dot_general | solution.py:31
  113.0 6.7 %fusion.22 = bf16[256,1,8,128]{0,3,2,1:T(8,128)(2,1)} fusion(f32[8,256]{1,0:T(8,128)S(1)} %fusion.73, bf16[256,2,128]{2,0,1:T(8,128)(2,1)} %fusion.23, bf16[1024,2,128]{2,0,1:T(8,128)(2,1)S(1)} %get-tuple-element.7, pred[256,1280]{0,1:T(8,128)(4,1)S(1)} %fusion.18, bf16[256,1,8,128]{3,2,1,0:T(8,128)(2,1)S(1)} %get-tuple-element.6, ...), kind=kOutput, calls=%fused_computation.28 | convolution fusion | flops 1356860672 | bytes 2695168 | tf_op jit(solution)/shard_map/grk,kd->rgd/dot_general | solution.py:31
  119.7 1.1 pad_maximum_fusion
  120.8 0.6 copy.32
  121.5 1.1 broadcast_select_fusion
  (22 shorter events, 0.1 us)
Async XLA Ops:
  0.0 10.2 %copy-start = (bf16[256,2048]{1,0:T(8,128)(2,1)S(1)}, bf16[256,2048]{1,0:T(8,128)(2,1)}, u32[]{:S(2)}) copy-start(bf16[256,2048]{1,0:T(8,128)(2,1)} %param.11) | copy-start | bytes 3145732
  0.0 8.3 %copy-start.7 = (s32[4]{0:T(128)S(1)}, s32[4]{0:T(128)}, u32[]{:S(2)}) copy-start(s32[4]{0:T(128)} %param.18) | copy-start | bytes 52
  0.0 10.2 %copy-start.5 = (bf16[2,32,2048]{2,1,0:T(8,128)(2,1)S(1)}, bf16[2,32,2048]{2,1,0:T(8,128)(2,1)}, u32[]{:S(2)}) copy-start(bf16[2,32,2048]{2,1,0:T(8,128)(2,1)} %param.15) | copy-start | bytes 786436
  1.5 20.3 %copy-start.2 = (bf16[256,2048]{1,0:T(8,128)(2,1)S(1)}, bf16[256,2048]{1,0:T(8,128)(2,1)}, u32[]{:S(2)}) copy-start(bf16[256,2048]{1,0:T(8,128)(2,1)} %param.12) | copy-start | bytes 3145732
  1.5 28.7 %collective-permute-start = (bf16[1024,2,256]{2,0,1:T(8,128)(2,1)S(1)}, bf16[1024,2,256]{2,0,1:T(8,128)(2,1)}, u32[]{:S(2)}, u32[]{:S(2)}) collective-permute-start(bf16[1024,2,256]{2,0,1:T(8,128)(2,1)S(1)} %bitcast.136), channel_id=1, source_target_pairs={{0,12},{4,0},{8,4},{12,8},{1,13},{5,1},{9,5},{13,9},{2,14},{6,2},{... | collective-permute-start | bytes 3145736 | tf_op jit(solution)/shard_map/ppermute | solution.py:14
  6.6 89.8 %collective-permute-start.1 = (bf16[1024,2,256]{2,0,1:T(8,128)(2,1)S(1)}, bf16[1024,2,256]{2,0,1:T(8,128)(2,1)}, u32[]{:S(2)}, u32[]{:S(2)}) collective-permute-start(bf16[1024,2,256]{2,0,1:T(8,128)(2,1)S(1)} %bitcast.137), channel_id=1, source_target_pairs={{0,8},{4,12},{8,0},{12,4},{1,9},{5,13},{9,1},{13,5},{2,10},{6,14},... | collective-permute-start | bytes 3145736 | tf_op jit(solution)/shard_map/ppermute | solution.py:14
  6.6 89.8 %collective-permute-start.2 = (bf16[1024,2,256]{2,0,1:T(8,128)(2,1)S(1)}, bf16[1024,2,256]{2,0,1:T(8,128)(2,1)}, u32[]{:S(2)}, u32[]{:S(2)}) collective-permute-start(bf16[1024,2,256]{2,0,1:T(8,128)(2,1)S(1)} %bitcast.138), channel_id=1, source_target_pairs={{0,4},{4,8},{8,12},{12,0},{1,5},{5,9},{9,13},{13,1},{2,6},{6,10},{... | collective-permute-start | bytes 3145736 | tf_op jit(solution)/shard_map/ppermute | solution.py:14
  23.0 1.0 copy-start.4
  23.1 1.8 %copy-start.6 = (bf16[2,16,2,128]{3,2,1,0:T(2,128)(2,1)S(1)}, bf16[2,16,2,128]{3,2,1,0:T(2,128)(2,1)}, u32[]{:S(2)}) copy-start(bf16[2,16,2,128]{3,2,1,0:T(2,128)(2,1)} %param.17) | copy-start | bytes 49156
  26.4 70.0 %copy-start.1 = (bf16[1,1024,2,256]{3,2,1,0:T(2,128)(2,1)S(1)}, bf16[1,1024,2,256]{3,2,1,0:T(2,128)(2,1)}, u32[]{:S(2)}) copy-start(bf16[1,1024,2,256]{3,2,1,0:T(2,128)(2,1)} %param.14) | copy-start | bytes 3145732
  113.0 6.7 %copy-start.3 = (bf16[256,1,8,128]{0,3,2,1:T(8,128)(2,1)S(1)}, bf16[256,1,8,128]{0,3,2,1:T(8,128)(2,1)}, u32[]{:S(2)}) copy-start(bf16[256,1,8,128]{0,3,2,1:T(8,128)(2,1)} %fusion.21) | copy-start | bytes 1572868
where the time goes:
time: 123 us
  waiting for transfers between devices  68.8 us (56%)
  matrix products  24.1 us (20%)
  blocking collectives  11.1 us (9%)
  starting transfers between devices  6.12 us (5%)
  other arithmetic  4.95 us (4%)
  local copies, waits for them, and re-layouts  4.76 us (4%)
  between operations  2.78 us (2%)
    ppermute x3, waiting for transfers between devices, passed_along(): lax.ppermute(shard, axis, [(i, (i + by) % size) for i in range(size)])  68.8 us
    dot_general x2, matrix products, attend(): jnp.einsum('grk,kd->rgd', weights, values, preferred_element_type=jnp.flo...  13.1 us
    psum x1, blocking collectives, on_device(): rank_projection = lax.psum(partial_low, 'tensor').astype(jnp.bfloat16)  11.1 us
    sub x2, matrix products, attend(): powers = jnp.exp(scores - largest)  8.47 us
    ppermute x3, starting transfers between devices, passed_along(): lax.ppermute(shard, axis, [(i, (i + by) % size) for i in range(size)])  6.12 us
    unnamed x19, local copies, waits for them, and re-layouts  3.09 us
  transfers between devices with their start and end apart: 3, of which 2 were waited for; matrix products, arithmetic and copies ran while one was open for 4% of the time, Pallas kernels for 0%

commit v1 on v0

v1 whole, which is shorter than its diff:
```python
import functools
import math

import jax
import jax.numpy as jnp
from jax import lax
from jax.experimental import pallas as pl
from jax.experimental.pallas import tpu as pltpu
from jax.sharding import PartitionSpec as P

STRETCH = 128
READ_SPAN = 4
VMEM_BYTES = 24 * 1024 * 1024
NT = (((1,), (1,)), ((), ()))
TN = (((0,), (0,)), ((), ()))


def swap_sum(value, axis):
    size = lax.axis_size(axis)
    if size & (size - 1):
        return lax.psum(value, axis)
    step = 1
    while step < size:
        value = value + lax.ppermute(value, axis, [(i, i ^ step) for i in range(size)])
        step *= 2
    return value


def head_scores(query, keys):
    return lax.dot_general(query, keys, NT, preferred_element_type=jnp.float32)


def with_ones(values):
    return jnp.concatenate([values, jnp.ones_like(values)], axis=1)


def wide(column, count):
    return jnp.concatenate([column] * count, axis=1) if count > 1 else column


def owner_of(places_ref, tenant_ref):
    return places_ref[tenant_ref[0]]


def copy_read(flags, page_ref, at, sources):
    for flag, source in zip(flags, sources):

        @pl.when(flag)
        def _():
            page_ref[at, :] = source[...]


def attend_part(shape, query_ref, at, keys, both, state, seen=None):
    heads, group, width, rank, scale = shape
    rows, depth = query_ref.shape[0], keys.shape[0]
    scores = head_scores(query_ref[:, at], keys)
    if seen is not None:
        scores = jnp.where(seen, scores, -jnp.inf)
    largest = jnp.broadcast_to(jnp.max(scores, axis=1, keepdims=True), (rows, width))
    if state is not None:
        before, weighted_before, total_before = state
        largest = jnp.maximum(before, largest)
        fade = jnp.exp2((before - largest) * scale)
    powers = jnp.exp2((scores - wide(largest, depth // width)) * scale)
    summed = jnp.dot(powers.astype(jnp.bfloat16), both, preferred_element_type=jnp.float32)
    weighted, total = summed[:, :width], summed[:, width:]
    if state is not None:
        weighted, total = weighted + weighted_before * fade, total + total_before * fade
    return largest, weighted, total


def first_kernel(shape, read_flags, cuts, routes, *refs):
    heads, group, width, rank, scale = shape
    places_ref, tenant_ref, choice_ref, low_ref, base_ref, up_query_ref, up_value_ref, suffix_ref = refs[:8]
    sources, (query_ref, largest_ref, weighted_ref, total_ref, page_ref) = refs[8:-5], refs[-5:]
    rows = base_ref.shape[0]
    choice = choice_ref[0]
    low = low_ref[...].astype(jnp.bfloat16)
    update = lax.dot_general(low[:rank], up_query_ref[choice], TN, preferred_element_type=jnp.float32)
    query_ref[...] = (base_ref[...].astype(jnp.float32) + update).astype(jnp.bfloat16)
    delta = lax.dot_general(low[rank:], up_value_ref[choice], TN, preferred_element_type=jnp.float32)
    flags = read_flags(owner_of(places_ref, tenant_ref))
    for part, (begin, end) in enumerate(cuts):
        copy_read(flags, page_ref, slice(begin, end), sources[part * routes : (part + 1) * routes])
    row = lax.broadcasted_iota(jnp.int32, (rows, rows), 0)
    column = lax.broadcasted_iota(jnp.int32, (rows, rows), 1)
    seen = column <= row
    for head in range(heads):
        start = 2 * width * head
        base_value = suffix_ref[:, start + width : start + 2 * width].astype(jnp.float32)
        values = (base_value + delta[:, head * width : (head + 1) * width]).astype(jnp.bfloat16)
        both = with_ones(values)
        page_both = with_ones(page_ref[:, start + width : start + 2 * width])
        for member in range(group):
            at = slice((head * group + member) * width, (head * group + member + 1) * width)
            state = attend_part(shape, query_ref, at, suffix_ref[:, start : start + width], both, None, seen)
            state = attend_part(shape, query_ref, at, page_ref[:, start : start + width], page_both, state)
            largest_ref[:, at], weighted_ref[:, at], total_ref[:, at] = state


def last_kernel(shape, read_flags, *refs):
    heads, group, width, rank, scale = shape
    places_ref, tenant_ref, blocks_ref, query_ref, largest_ref, weighted_ref, total_ref = refs[:7]
    sources, (out_ref, page_ref) = refs[7:-2], refs[-2:]
    rows = query_ref.shape[0]
    flags = read_flags(owner_of(places_ref, tenant_ref))
    copy_read(flags, page_ref, slice(0, page_ref.shape[0]), sources)
    live = lax.broadcasted_iota(jnp.int32, (rows, width), 0) < blocks_ref[0] * STRETCH
    for head in range(heads):
        start = 2 * width * head
        both = with_ones(page_ref[:, start + width : start + 2 * width])
        for member in range(group):
            at = slice((head * group + member) * width, (head * group + member + 1) * width)
            state = largest_ref[:, at], weighted_ref[:, at], total_ref[:, at]
            keys = page_ref[:, start : start + width]
            largest, weighted, total = attend_part(shape, query_ref, at, keys, both, state)
            out_ref[:, at] = jnp.where(live, weighted / total, 0.0).astype(jnp.bfloat16)


def wish_kernel(places_ref, tenant_ref, out_ref):
    other_end = jnp.where(lax.axis_index("replica") >= 2, 0, 3)
    wished = jnp.where(owner_of(places_ref, tenant_ref) == other_end, 1.0, 0.0)
    out_ref[...] = jnp.full(out_ref.shape, wished, jnp.float32)


def in_vmem(array):
    return pltpu.with_memory_space_constraint(array, pltpu.VMEM)


WHOLE = pl.BlockSpec(memory_space=pltpu.VMEM)
SCALARS = pl.BlockSpec(memory_space=pltpu.SMEM)


def cost(rows, columns, keys):
    return pl.CostEstimate(
        flops=4 * rows * columns * keys, bytes_accessed=4 * rows * columns, transcendentals=0
    )


def attend_first(shape, read_flags, scalars, inputs, parts):
    rows, columns = inputs[1].shape
    depths = [sources[0].shape[0] for sources in parts]
    cuts = [(sum(depths[:k]), sum(depths[: k + 1])) for k in range(len(depths))]
    state = pltpu.VMEM((rows, columns), jnp.float32)
    sources = [source for sources in parts for source in sources]
    return pl.pallas_call(
        functools.partial(first_kernel, shape, read_flags, cuts, len(parts[0])),
        out_shape=(pltpu.VMEM((rows, columns), jnp.bfloat16), state, state, state),
        in_specs=[SCALARS] * 3 + [WHOLE] * (5 + len(sources)),
        out_specs=(WHOLE,) * 4,
        scratch_shapes=[pltpu.VMEM((sum(depths), sources[0].shape[1]), jnp.bfloat16)],
        compiler_params=pltpu.CompilerParams(vmem_limit_bytes=VMEM_BYTES),
        cost_estimate=cost(rows, columns, sum(depths) + rows),
        name="attend_first",
    )(*scalars, *inputs, *sources)


def attend_last(shape, read_flags, scalars, states, sources):
    rows, columns = states[0].shape
    return pl.pallas_call(
        functools.partial(last_kernel, shape, read_flags),
        out_shape=jax.ShapeDtypeStruct((rows, columns), jnp.bfloat16),
        in_specs=[SCALARS] * 3 + [WHOLE] * (4 + len(sources)),
        out_specs=WHOLE,
        scratch_shapes=[pltpu.VMEM(sources[0].shape, jnp.bfloat16)],
        compiler_params=pltpu.CompilerParams(vmem_limit_bytes=VMEM_BYTES),
        cost_estimate=cost(rows, columns, sources[0].shape[0]),
        name="attend_last",
    )(*scalars, *map(in_vmem, states), *sources)


def wish(places, tenant, columns):
    return pl.pallas_call(
        wish_kernel,
        out_shape=jax.ShapeDtypeStruct((1, columns), jnp.float32),
        in_specs=[SCALARS] * 2,
        out_specs=WHOLE,
        name="wish",
    )(places, tenant)


EDGES, MIDDLE, FAR = [(0, 1), (1, 0), (2, 3), (3, 2)], [(1, 2), (2, 1)], [(1, 3), (2, 0)]
TO_INSIDE = [(3, 1), (0, 2)]
PARTS = (1, 2, 3, 2)


def moved(chunk, pairs):
    return lax.ppermute(chunk, "replica", pairs)


def line_flags(owner):
    place = lax.axis_index("replica")
    beside = jnp.where(place < 2, 1 - place, 5 - place)
    inside = (place == 1) | (place == 2)
    other = (owner != place) & (owner != beside)
    return owner == place, owner == beside, other & inside, other & jnp.logical_not(inside)


def line_attention(shape, page, places, tenant, blocks, low_of, inputs):
    count = len(PARTS)
    unit = page.shape[0] // sum(PARTS)
    page = page.reshape(page.shape[0], -1)
    own = [page[unit * sum(PARTS[:k]) : unit * sum(PARTS[: k + 1])] for k in range(count)]
    wished = wish(places, tenant, page.shape[1])
    wish_middle = moved(wished, MIDDLE)
    wish_far = moved(wished, TO_INSIDE)
    edge = [moved(own[k], EDGES) for k in range(count)]
    low = low_of()
    middle, far = [], []
    for k in range(count):
        middle.append(moved(jnp.where(wish_middle > 0, edge[k], own[k]), MIDDLE))
        far.append(moved(jnp.where(wish_far > 0, edge[k], own[k]), FAR))
    sources = list(zip(own, edge, middle, far))
    states = attend_first(
        shape, line_flags, (places, tenant, inputs[0]), (low, *inputs[1:]), sources[:-1]
    )
    return attend_last(shape, line_flags, (places, tenant, blocks), states, sources[-1])


def ring_attention(shape, page, places, tenant, blocks, low_of, inputs):
    size = lax.axis_size("replica")

    def read_flags(owner):
        place = lax.axis_index("replica")
        distance = jnp.where(owner > place, place - owner + size, place - owner)
        return [distance == offset for offset in range(READ_SPAN)]

    page = page.reshape(page.shape[0], -1)
    cut = page.shape[0] * 3 // 4
    shifts = [[(i, (i + by) % size) for i in range(size)] for by in range(1, READ_SPAN)]
    parts = [[part] + [moved(part, pairs) for pairs in shifts] for part in (page[:cut], page[cut:])]
    states = attend_first(
        shape, read_flags, (places, tenant, inputs[0]), (low_of(), *inputs[1:]), parts[:1]
    )
    return attend_last(shape, read_flags, (places, tenant, blocks), states, parts[1])


def on_device(
    suffix_hidden,
    base_query,
    suffix_key_value,
    tenant_prefix_cache,
    adapter_down,
    adapter_up_query,
    adapter_up_value,
    tenant_replica,
    tenant_of_request,
    suffix_blocks,
    request_adapter,
):
    rows = suffix_hidden.shape[0]
    heads, width = suffix_key_value.shape[1], suffix_key_value.shape[2] // 2
    group = base_query.shape[1] // (heads * width)
    adapters, rank = adapter_down.shape[0], adapter_down.shape[1] // 2
    shape = (heads, group, width, rank, math.log2(math.e) / math.sqrt(width))

    def low_of():
        down = lax.dynamic_index_in_dim(adapter_down, request_adapter[0], 0, keepdims=False)
        low = lax.dot_general(down, suffix_hidden, NT, preferred_element_type=jnp.float32)
        return swap_sum(low, "tensor")

    inputs = (
        request_adapter,
        base_query,
        adapter_up_query,
        adapter_up_value.reshape(adapters, rank, heads * width),
        suffix_key_value.reshape(rows, heads * 2 * width),
    )
    attention = line_attention if lax.axis_size("replica") == 4 else ring_attention
    return attention(
        shape, tenant_prefix_cache[0], tenant_replica, tenant_of_request, suffix_blocks,
        low_of, inputs,
    )


def solution(mesh):
    in_specs = (
        P(("group", "replica"), "tensor"),
        P(("group", "replica"), "tensor"),
        P(("group", "replica"), "tensor", None),
        P(("group", "replica"), None, "tensor", None),
        P(None, None, "tensor"),
        P(None, None, "tensor"),
        P(None, None, "tensor", None),
        P("group"),
        P(("group", "replica")),
        P(("group", "replica")),
        P(("group", "replica")),
    )
    out_specs = P(("group", "replica"), "tensor")
    return jax.shard_map(
        on_device, mesh=mesh, in_specs=in_specs, out_specs=out_specs, check_vma=False
    )
```

time: 123 us -> 99.1 us (0.81)
  waiting for transfers between devices: 68.8 us -> 43.6 us
  matrix products: 24.1 us -> 1.32 us
  starting transfers between devices: 6.12 us -> 21 us
  Pallas kernels: 0 us -> 14.2 us
  blocking collectives: 11.1 us -> 0 us
  local copies, waits for them, and re-layouts: 4.76 us -> 12.4 us
  other arithmetic: 4.95 us -> 2.82 us
    ppermute x3 -> x16, waiting for transfers between devices: 68.8 us -> 43.6 us  [the longest x14 41.2 us: moved(): return lax.ppermute(chunk, 'replica', pairs)]
    ppermute x3 -> x16, starting transfers between devices: 6.12 us -> 21 us  [the longest x14 19.4 us: moved(): return lax.ppermute(chunk, 'replica', pairs)]
    dot_general x5 -> x1, matrix products: 15.6 us -> 1.32 us  [low_of(): lax.dot_general(down, suffix_hidden, NT, preferred_element_type=jnp.float32)]
    pallas_call x0 -> x3, Pallas kernels: none -> 14.2 us  [the longest x1 9.29 us: attend_first(): pl.pallas_call(functools.partial(first_kernel, shape, read_flags, cuts, l...]
    psum x1 -> x0, blocking collectives: 11.1 us -> none  [on_device(): rank_projection = lax.psum(partial_low, 'tensor').astype(jnp.bfloat16)]
    sub x2 -> x0, matrix products: 8.47 us -> none  [attend(): powers = jnp.exp(scores - largest)]
    unnamed x19 -> x39, local copies, waits for them, and re-layouts: 3.09 us -> 10.2 us
    select_n x2 -> x3, other arithmetic: 2.67 us -> 1.99 us  [line_attention(): far.append(moved(jnp.where(wish_far > 0, edge[k], own[k]), FAR))]
  transfers between devices with their start and end apart: 3 -> 16, of which waited for: 2 -> 4; matrix products, arithmetic and copies ran while one was open for 4% -> 7% of each run, Pallas kernels for 0% -> 10%
where the time goes in v1:
time: 99.1 us; the launch traced here: 97.7 us
  waiting for transfers between devices  43.6 us (44%)
  starting transfers between devices  21 us (21%)
  Pallas kernels  14.2 us (14%)
  local copies, waits for them, and re-layouts  12.4 us (13%)
  other arithmetic  2.82 us (3%)
  between operations  2.41 us (2%)
  matrix products  1.32 us (1%)
    ppermute x14, waiting for transfers between devices, moved(): return lax.ppermute(chunk, 'replica', pairs)  41.2 us
    ppermute x14, starting transfers between devices, moved(): return lax.ppermute(chunk, 'replica', pairs)  19.4 us
    unnamed x39, local copies, waits for them, and re-layouts  10.2 us
    pallas_call x1, Pallas kernels, attend_first(): pl.pallas_call(functools.partial(first_kernel, shape, read_flags, cuts, l...  9.29 us
    pallas_call x1, Pallas kernels, attend_last(): pl.pallas_call(functools.partial(last_kernel, shape, read_flags), out_sha...  3.61 us
    ppermute x2, waiting for transfers between devices, swap_sum(): lax.ppermute(value, axis, [(i, i ^ step) for i in range(size)])  2.43 us
    select_n x3, other arithmetic, line_attention(): far.append(moved(jnp.where(wish_far > 0, edge[k], own[k]), FAR))  1.99 us
  transfers between devices with their start and end apart: 16, of which 4 were waited for; matrix products, arithmetic and copies ran while one was open for 7% of the time, Pallas kernels for 10%

profile of v1, /device:TPU:0, one launch (start us, length us, event | category | flops | bytes accessed | tf_op | source)
XLA Modules:
  0.0 97.7 jit_solution(16882596014886067165)
XLA Ops:
  0.8 1.3 %wish.1 = f32[1,512]{1,0:T(1,128)} custom-call(s32[4]{0:T(128)} %refs_0_.3, s32[1]{0:T(128)S(6)} %copy.17.tenant_ref.refs_1_), custom_call_target="tpu_custom_call" | custom-call | tf_op jit(solution)/shard_map/wish/pallas_call | solution.py:173
  2.0 5.9 %collective-permute-start.5 = (f32[1,512]{1,0:T(1,128)}, f32[1,512]{1,0:T(1,128)S(1)}, u32[]{:S(2)}, u32[]{:S(2)}) collective-permute-start(f32[1,512]{1,0:T(1,128)} %wish.1), channel_id=1, source_target_pairs={{12,4},{0,8},{13,5},{1,9},{14,6},{2,10},{15,7},{3,11},{28,20},{16,... | collective-permute-start | bytes 6152 | tf_op jit(solution)/shard_map/ppermute | solution.py:188
  9.3 1.3 %fusion = f32[32,256]{1,0:T(8,128)S(1)} fusion(bf16[256,2048]{1,0:T(8,128)(2,1)S(1)} %copy-done, bf16[2,32,2048]{2,1,0:T(8,128)(2,1)} %param.15, s32[]{:T(128)S(6)} %select_n.31), kind=kOutput, calls=%fused_computation.6 | convolution fusion | flops 33554432 | bytes 1212420 | tf_op jit(solution)/shard_map/dot_general | solution.py:259
  10.7 1.4 %fusion.4 = (bf16[1,256,2,256]{3,2,1,0:T(2,128)(2,1)S(1)}, bf16[1,256,2,256]{3,2,1,0:T(2,128)(2,1)S(1)}) fusion(bf16[1,1024,2,256]{3,2,1,0:T(2,128)(2,1)} %param.14), kind=kLoop, calls=%fused_computation.14 | loop fusion | bytes 1048576 | tf_op jit(solution)/shard_map/slice | solution.py:203
  12.1 1.3 %collective-permute-start.13 = (bf16[256,512]{1,0:T(8,128)(2,1)S(1)}, bf16[256,512]{1,0:T(8,128)(2,1)S(1)}, u32[]{:S(2)}, u32[]{:S(2)}) collective-permute-start(bf16[256,512]{1,0:T(8,128)(2,1)S(1)} %bitcast.22), channel_id=1, source_target_pairs={{0,4},{4,0},{8,12},{12,8},{1,5},{5,1},{9,13},{13,9},{2,6},{6,2},{1... | collective-permute-start | bytes 786440 | tf_op jit(solution)/shard_map/ppermute | solution.py:188
  14.4 1.3 %collective-permute-start.2 = (bf16[128,512]{1,0:T(8,128)(2,1)S(1)}, bf16[128,512]{1,0:T(8,128)(2,1)S(1)}, u32[]{:S(2)}, u32[]{:S(2)}) collective-permute-start(bf16[128,512]{1,0:T(8,128)(2,1)S(1)} %bitcast.31), channel_id=1, source_target_pairs={{0,4},{4,0},{8,12},{12,8},{1,5},{5,1},{9,13},{13,9},{2,6},{6,2},{1... | collective-permute-start | bytes 393224 | tf_op jit(solution)/shard_map/ppermute | solution.py:188
  16.7 15.9 %collective-permute-done.2.refs_9_ = bf16[128,512]{1,0:T(8,128)(2,1)S(1)} collective-permute-done((bf16[128,512]{1,0:T(8,128)(2,1)S(1)}, bf16[128,512]{1,0:T(8,128)(2,1)S(1)}, u32[]{:S(2)}, u32[]{:S(2)}) %collective-permute-start.2) | collective-permute-done | bytes 131104 | tf_op jit(solution)/shard_map/ppermute | solution.py:188
  33.9 1.0 broadcast_select_fusion
  34.8 1.4 %collective-permute-start.11 = (bf16[384,512]{1,0:T(8,128)(2,1)}, bf16[384,512]{1,0:T(8,128)(2,1)}, u32[]{:S(2)}, u32[]{:S(2)}) collective-permute-start(bf16[384,512]{1,0:T(8,128)(2,1)} %get-tuple-element.16), channel_id=1, source_target_pairs={{4,8},{8,4},{5,9},{9,5},{6,10},{10,6},{7,11},{11,7},{20,24},{24,20... | collective-permute-start | bytes 1179656 | tf_op jit(solution)/shard_map/ppermute | solution.py:188
  36.2 1.3 %collective-permute-start.12 = (bf16[384,512]{1,0:T(8,128)(2,1)}, bf16[384,512]{1,0:T(8,128)(2,1)}, u32[]{:S(2)}, u32[]{:S(2)}) collective-permute-start(bf16[384,512]{1,0:T(8,128)(2,1)} %get-tuple-element.15), channel_id=1, source_target_pairs={{4,12},{8,0},{5,13},{9,1},{6,14},{10,2},{7,15},{11,3},{20,28},{24,... | collective-permute-start | bytes 1179656 | tf_op jit(solution)/shard_map/ppermute | solution.py:188
  37.8 1.0 %broadcast_select_fusion.3 = (bf16[256,512]{1,0:T(8,128)(2,1)}, bf16[256,512]{1,0:T(8,128)(2,1)S(1)}, bf16[256,512]{1,0:T(8,128)(2,1)}, bf16[256,512]{1,0:T(8,128)(2,1)}) fusion(bf16[256,512]{1,0:T(8,128)(2,1)S(1)} %collective-permute-done.7.refs_13_, bf16[256,512]{1,0:T(8,128)(2,1)S(1)} %bitcast.29, pred[512]{0:T(512)(128)(4,1)S(1)} %compare_reduce_fusion, ...), kind=kLoop, calls=%fused_computation.3 | loop fusion | flops 524288 | bytes 2098176 | tf_op jit(solution)/shard_map/jit(_where)/select_n | solution.py:212
  39.5 1.6 %collective-permute-start.1 = (f32[32,256]{1,0:T(8,128)S(1)}, f32[32,256]{1,0:T(8,128)S(1)}, u32[]{:S(2)}, u32[]{:S(2)}) collective-permute-start(f32[32,256]{1,0:T(8,128)S(1)} %add.11), channel_id=1, source_target_pairs={{0,2},{1,3},{2,0},{3,1},{4,6},{5,7},{6,4},{7,5},{8,10},{9,11},{10,... | collective-permute-start | bytes 98312 | tf_op jit(solution)/shard_map/ppermute | solution.py:24
  41.1 2.4 %collective-permute-done.1 = f32[32,256]{1,0:T(8,128)S(1)} collective-permute-done((f32[32,256]{1,0:T(8,128)S(1)}, f32[32,256]{1,0:T(8,128)S(1)}, u32[]{:S(2)}, u32[]{:S(2)}) %collective-permute-start.1) | collective-permute-done | bytes 32800 | tf_op jit(solution)/shard_map/ppermute | solution.py:24
  43.5 1.3 %collective-permute-start.9 = (bf16[256,512]{1,0:T(8,128)(2,1)}, bf16[256,512]{1,0:T(8,128)(2,1)}, u32[]{:S(2)}, u32[]{:S(2)}) collective-permute-start(bf16[256,512]{1,0:T(8,128)(2,1)} %get-tuple-element.19), channel_id=1, source_target_pairs={{4,12},{8,0},{5,13},{9,1},{6,14},{10,2},{7,15},{11,3},{20,28},{24,... | collective-permute-start | bytes 786440 | tf_op jit(solution)/shard_map/ppermute | solution.py:188
  45.4 1.3 %collective-permute-start.6 = (bf16[128,512]{1,0:T(8,128)(2,1)S(1)}, bf16[128,512]{1,0:T(8,128)(2,1)S(1)}, u32[]{:S(2)}, u32[]{:S(2)}) collective-permute-start(bf16[128,512]{1,0:T(8,128)(2,1)S(1)} %get-tuple-element.21), channel_id=1, source_target_pairs={{4,12},{8,0},{5,13},{9,1},{6,14},{10,2},{7,15},{11,3},{20,28},{24,... | collective-permute-start | bytes 393224 | tf_op jit(solution)/shard_map/ppermute | solution.py:188
  46.7 25.1 %collective-permute-done.6.refs_11_ = bf16[128,512]{1,0:T(8,128)(2,1)S(1)} collective-permute-done((bf16[128,512]{1,0:T(8,128)(2,1)S(1)}, bf16[128,512]{1,0:T(8,128)(2,1)S(1)}, u32[]{:S(2)}, u32[]{:S(2)}) %collective-permute-start.6) | collective-permute-done | bytes 131104 | tf_op jit(solution)/shard_map/ppermute | solution.py:188
  73.8 1.3 %collective-permute-start.15 = (bf16[256,512]{1,0:T(8,128)(2,1)}, bf16[256,512]{1,0:T(8,128)(2,1)S(1)}, u32[]{:S(2)}, u32[]{:S(2)}) collective-permute-start(bf16[256,512]{1,0:T(8,128)(2,1)} %get-tuple-element.24), channel_id=1, source_target_pairs={{4,12},{8,0},{5,13},{9,1},{6,14},{10,2},{7,15},{11,3},{20,28},{24,... | collective-permute-start | bytes 786440 | tf_op jit(solution)/shard_map/ppermute | solution.py:188
  77.4 0.9 copy-done.2
  78.4 0.9 copy-done.4
  79.9 1.2 %copy-done.6 = bf16[256,2048]{1,0:T(8,128)(2,1)S(1)} copy-done((bf16[256,2048]{1,0:T(8,128)(2,1)S(1)}, bf16[256,2048]{1,0:T(8,128)(2,1)}, u32[]{:S(2)}) %copy-start.6) | copy-done | bytes 1048600
  81.1 0.9 copy-done.8
  82.1 0.9 copy-done.9
  84.8 9.3 %attend_first.1 = (bf16[256,2048]{1,0:T(8,128)(2,1)S(1)}, f32[256,2048]{1,0:T(8,128)S(1)}, f32[256,2048]{1,0:T(8,128)S(1)}, f32[256,2048]{1,0:T(8,128)S(1)}) custom-call(s32[4]{0:T(128)S(1)} %copy-done.5, s32[1]{0:T(128)S(6)} %copy.17.tenant_ref.refs_1_, s32[1]{0:T(128)} %copy.19.refs_2_, f32[32,256]{1,0:T(8,128)S(1)} %add.12.refs_3_, ...), custom_call_target="tpu_custom_call" | custom-call | flops 2147483648 | bytes 2097152 | tf_op jit(solution)/shard_map/attend_first/pallas_call | solution.py:146
  94.1 3.6 %attend_last.1 = bf16[256,2048]{1,0:T(8,128)(2,1)} custom-call(s32[4]{0:T(128)S(1)} %copy-done.5, s32[1]{0:T(128)S(6)} %copy.17.tenant_ref.refs_1_, s32[1]{0:T(128)S(6)} %copy.18.refs_2_, bf16[256,2048]{1,0:T(8,128)(2,1)S(1)} %get-tuple-element.9.refs_3_, f32[256,2048]{1,0:T(8,128)S(1)} %get-tuple-element.10.refs_4_, ...), custom_call_target="tpu_custom_call" | custom-call | flops 536870912 | bytes 2097152 | tf_op jit(solution)/shard_map/attend_last/pallas_call | solution.py:160
  (64 shorter events, 11.7 us)
Async XLA Ops:
  0.0 9.3 %copy-start = (bf16[256,2048]{1,0:T(8,128)(2,1)S(1)}, bf16[256,2048]{1,0:T(8,128)(2,1)}, u32[]{:S(2)}) copy-start(bf16[256,2048]{1,0:T(8,128)(2,1)} %param.11) | copy-start | bytes 3145732
  0.0 13.4 %slice-start = ((bf16[1,1024,2,256]{3,2,1,0:T(2,128)(2,1)}), bf16[1,384,2,256]{3,2,1,0:T(2,128)(2,1)S(1)}, s32[]{:S(2)}) async-start(bf16[1,1024,2,256]{3,2,1,0:T(2,128)(2,1)} %param.14), calls=%async_computation | async-start | bytes 786432 | tf_op jit(solution)/shard_map/slice | solution.py:203
  2.0 12.4 %collective-permute-start.5 = (f32[1,512]{1,0:T(1,128)}, f32[1,512]{1,0:T(1,128)S(1)}, u32[]{:S(2)}, u32[]{:S(2)}) collective-permute-start(f32[1,512]{1,0:T(1,128)} %wish.1), channel_id=1, source_target_pairs={{12,4},{0,8},{13,5},{1,9},{14,6},{2,10},{15,7},{3,11},{28,20},{16,... | collective-permute-start | bytes 6152 | tf_op jit(solution)/shard_map/ppermute | solution.py:188
  8.0 7.8 %collective-permute-start.3 = (f32[1,512]{1,0:T(1,128)}, f32[1,512]{1,0:T(1,128)S(1)}, u32[]{:S(2)}, u32[]{:S(2)}) collective-permute-start(f32[1,512]{1,0:T(1,128)} %wish.1), channel_id=1, source_target_pairs={{4,8},{8,4},{5,9},{9,5},{6,10},{10,6},{7,11},{11,7},{20,24},{24,20... | collective-permute-start | bytes 6152 | tf_op jit(solution)/shard_map/ppermute | solution.py:188
  10.6 3.8 %slice-start.1 = ((bf16[1,1024,2,256]{3,2,1,0:T(2,128)(2,1)}), bf16[1,128,2,256]{3,2,1,0:T(2,128)(2,1)S(1)}, s32[]{:S(2)}) async-start(bf16[1,1024,2,256]{3,2,1,0:T(2,128)(2,1)} %param.14), calls=%async_computation.1 | async-start | bytes 262144 | tf_op jit(solution)/shard_map/slice | solution.py:203
  10.6 28.8 %collective-permute-start = (f32[32,256]{1,0:T(8,128)S(1)}, f32[32,256]{1,0:T(8,128)S(1)}, u32[]{:S(2)}, u32[]{:S(2)}) collective-permute-start(f32[32,256]{1,0:T(8,128)S(1)} %fusion), channel_id=1, source_target_pairs={{0,1},{1,0},{2,3},{3,2},{4,5},{5,4},{6,7},{7,6},{8,9},{9,8},{10,11... | collective-permute-start | bytes 98312 | tf_op jit(solution)/shard_map/ppermute | solution.py:24
  12.1 24.1 %collective-permute-start.13 = (bf16[256,512]{1,0:T(8,128)(2,1)S(1)}, bf16[256,512]{1,0:T(8,128)(2,1)S(1)}, u32[]{:S(2)}, u32[]{:S(2)}) collective-permute-start(bf16[256,512]{1,0:T(8,128)(2,1)S(1)} %bitcast.22), channel_id=1, source_target_pairs={{0,4},{4,0},{8,12},{12,8},{1,5},{5,1},{9,13},{13,9},{2,6},{6,2},{1... | collective-permute-start | bytes 786440 | tf_op jit(solution)/shard_map/ppermute | solution.py:188
  13.5 20.4 %collective-permute-start.10 = (bf16[384,512]{1,0:T(8,128)(2,1)S(1)}, bf16[384,512]{1,0:T(8,128)(2,1)S(1)}, u32[]{:S(2)}, u32[]{:S(2)}) collective-permute-start(bf16[384,512]{1,0:T(8,128)(2,1)S(1)} %bitcast.25), channel_id=1, source_target_pairs={{0,4},{4,0},{8,12},{12,8},{1,5},{5,1},{9,13},{13,9},{2,6},{6,2},{1... | collective-permute-start | bytes 1179656 | tf_op jit(solution)/shard_map/ppermute | solution.py:188
  14.4 18.1 %collective-permute-start.2 = (bf16[128,512]{1,0:T(8,128)(2,1)S(1)}, bf16[128,512]{1,0:T(8,128)(2,1)S(1)}, u32[]{:S(2)}, u32[]{:S(2)}) collective-permute-start(bf16[128,512]{1,0:T(8,128)(2,1)S(1)} %bitcast.31), channel_id=1, source_target_pairs={{0,4},{4,0},{8,12},{12,8},{1,5},{5,1},{9,13},{13,9},{2,6},{6,2},{1... | collective-permute-start | bytes 393224 | tf_op jit(solution)/shard_map/ppermute | solution.py:188
  15.7 22.0 %collective-permute-start.7 = (bf16[256,512]{1,0:T(8,128)(2,1)S(1)}, bf16[256,512]{1,0:T(8,128)(2,1)S(1)}, u32[]{:S(2)}, u32[]{:S(2)}) collective-permute-start(bf16[256,512]{1,0:T(8,128)(2,1)S(1)} %bitcast.28), channel_id=1, source_target_pairs={{0,4},{4,0},{8,12},{12,8},{1,5},{5,1},{9,13},{13,9},{2,6},{6,2},{1... | collective-permute-start | bytes 786440 | tf_op jit(solution)/shard_map/ppermute | solution.py:188
  16.7 58.5 %copy-start.14 = (bf16[256,2,256]{2,1,0:T(2,128)(2,1)S(1)}, bf16[256,2,256]{2,1,0:T(2,128)(2,1)}, u32[]{:S(2)}) copy-start(bf16[256,2,256]{2,1,0:T(2,128)(2,1)} %param.13) | copy-start | bytes 786436
  33.2 11.6 %collective-permute-start.4 = (bf16[128,512]{1,0:T(8,128)(2,1)S(1)}, bf16[128,512]{1,0:T(8,128)(2,1)S(1)}, u32[]{:S(2)}, u32[]{:S(2)}) collective-permute-start(bf16[128,512]{1,0:T(8,128)(2,1)S(1)} %get-tuple-element.22), channel_id=1, source_target_pairs={{4,8},{8,4},{5,9},{9,5},{6,10},{10,6},{7,11},{11,7},{20,24},{24,20... | collective-permute-start | bytes 393224 | tf_op jit(solution)/shard_map/ppermute | solution.py:188
  34.8 42.6 %collective-permute-start.11 = (bf16[384,512]{1,0:T(8,128)(2,1)}, bf16[384,512]{1,0:T(8,128)(2,1)}, u32[]{:S(2)}, u32[]{:S(2)}) collective-permute-start(bf16[384,512]{1,0:T(8,128)(2,1)} %get-tuple-element.16), channel_id=1, source_target_pairs={{4,8},{8,4},{5,9},{9,5},{6,10},{10,6},{7,11},{11,7},{20,24},{24,20... | collective-permute-start | bytes 1179656 | tf_op jit(solution)/shard_map/ppermute | solution.py:188
  36.2 41.2 %collective-permute-start.12 = (bf16[384,512]{1,0:T(8,128)(2,1)}, bf16[384,512]{1,0:T(8,128)(2,1)}, u32[]{:S(2)}, u32[]{:S(2)}) collective-permute-start(bf16[384,512]{1,0:T(8,128)(2,1)} %get-tuple-element.15), channel_id=1, source_target_pairs={{4,12},{8,0},{5,13},{9,1},{6,14},{10,2},{7,15},{11,3},{20,28},{24,... | collective-permute-start | bytes 1179656 | tf_op jit(solution)/shard_map/ppermute | solution.py:188
  37.8 37.4 %copy-start.1 = (bf16[256,512]{1,0:T(8,128)(2,1)}, bf16[256,512]{1,0:T(8,128)(2,1)S(1)}, u32[]{:S(2)}) copy-start(bf16[256,512]{1,0:T(8,128)(2,1)S(1)} %collective-permute-done.7.refs_13_) | copy-start | bytes 786436
  38.8 34.3 %collective-permute-start.8 = (bf16[256,512]{1,0:T(8,128)(2,1)S(1)}, bf16[256,512]{1,0:T(8,128)(2,1)S(1)}, u32[]{:S(2)}, u32[]{:S(2)}) collective-permute-start(bf16[256,512]{1,0:T(8,128)(2,1)S(1)} %get-tuple-element.20), channel_id=1, source_target_pairs={{4,8},{8,4},{5,9},{9,5},{6,10},{10,6},{7,11},{11,7},{20,24},{24,20... | collective-permute-start | bytes 786440 | tf_op jit(solution)/shard_map/ppermute | solution.py:188
  39.5 5.3 %copy-start.15 = (f32[32,256]{1,0:T(8,128)}, f32[32,256]{1,0:T(8,128)S(1)}, u32[]{:S(2)}) copy-start(f32[32,256]{1,0:T(8,128)S(1)} %add.11) | copy-start | bytes 98308
  39.5 4.0 %collective-permute-start.1 = (f32[32,256]{1,0:T(8,128)S(1)}, f32[32,256]{1,0:T(8,128)S(1)}, u32[]{:S(2)}, u32[]{:S(2)}) collective-permute-start(f32[32,256]{1,0:T(8,128)S(1)} %add.11), channel_id=1, source_target_pairs={{0,2},{1,3},{2,0},{3,1},{4,6},{5,7},{6,4},{7,5},{8,10},{9,11},{10,... | collective-permute-start | bytes 98312 | tf_op jit(solution)/shard_map/ppermute | solution.py:24
  43.5 31.7 %copy-start.16 = (f32[32,256]{1,0:T(8,128)}, f32[32,256]{1,0:T(8,128)S(1)}, u32[]{:S(2)}) copy-start(f32[32,256]{1,0:T(8,128)S(1)} %collective-permute-done.1) | copy-start | bytes 98308
  43.5 33.9 %collective-permute-start.9 = (bf16[256,512]{1,0:T(8,128)(2,1)}, bf16[256,512]{1,0:T(8,128)(2,1)}, u32[]{:S(2)}, u32[]{:S(2)}) collective-permute-start(bf16[256,512]{1,0:T(8,128)(2,1)} %get-tuple-element.19), channel_id=1, source_target_pairs={{4,12},{8,0},{5,13},{9,1},{6,14},{10,2},{7,15},{11,3},{20,28},{24,... | collective-permute-start | bytes 786440 | tf_op jit(solution)/shard_map/ppermute | solution.py:188
  45.4 26.3 %collective-permute-start.6 = (bf16[128,512]{1,0:T(8,128)(2,1)S(1)}, bf16[128,512]{1,0:T(8,128)(2,1)S(1)}, u32[]{:S(2)}, u32[]{:S(2)}) collective-permute-start(bf16[128,512]{1,0:T(8,128)(2,1)S(1)} %get-tuple-element.21), channel_id=1, source_target_pairs={{4,12},{8,0},{5,13},{9,1},{6,14},{10,2},{7,15},{11,3},{20,28},{24,... | collective-permute-start | bytes 393224 | tf_op jit(solution)/shard_map/ppermute | solution.py:188
  72.4 21.7 %collective-permute-start.14 = (bf16[256,512]{1,0:T(8,128)(2,1)}, bf16[256,512]{1,0:T(8,128)(2,1)S(1)}, u32[]{:S(2)}, u32[]{:S(2)}) collective-permute-start(bf16[256,512]{1,0:T(8,128)(2,1)} %get-tuple-element.23), channel_id=1, source_target_pairs={{4,8},{8,4},{5,9},{9,5},{6,10},{10,6},{7,11},{11,7},{20,24},{24,20... | collective-permute-start | bytes 786440 | tf_op jit(solution)/shard_map/ppermute | solution.py:188
  73.8 20.3 %collective-permute-start.15 = (bf16[256,512]{1,0:T(8,128)(2,1)}, bf16[256,512]{1,0:T(8,128)(2,1)S(1)}, u32[]{:S(2)}, u32[]{:S(2)}) collective-permute-start(bf16[256,512]{1,0:T(8,128)(2,1)} %get-tuple-element.24), channel_id=1, source_target_pairs={{4,12},{8,0},{5,13},{9,1},{6,14},{10,2},{7,15},{11,3},{20,28},{24,... | collective-permute-start | bytes 786440 | tf_op jit(solution)/shard_map/ppermute | solution.py:188
  79.9 1.2 %copy-start.6 = (bf16[256,2048]{1,0:T(8,128)(2,1)S(1)}, bf16[256,2048]{1,0:T(8,128)(2,1)}, u32[]{:S(2)}) copy-start(bf16[256,2048]{1,0:T(8,128)(2,1)} %refs_4_.1) | copy-start | bytes 3145732
  (11 other events, 8.9 us)

commit v2 on v1

--- a/solution.py
+++ b/solution.py
@@ -42,12 +42,14 @@
     return places_ref[tenant_ref[0]]
 
 
-def copy_read(flags, page_ref, at, sources):
+def fetch_read(flags, target, sources, semaphore):
     for flag, source in zip(flags, sources):
 
         @pl.when(flag)
         def _():
-            page_ref[at, :] = source[...]
+            pltpu.make_async_copy(source, target, semaphore).start()
+
+    return pltpu.make_async_copy(sources[0], target, semaphore)
 
 
 def attend_part(shape, query_ref, at, keys, both, state, seen=None):
@@ -72,19 +74,28 @@
 def first_kernel(shape, read_flags, cuts, routes, *refs):
     heads, group, width, rank, scale = shape
     places_ref, tenant_ref, choice_ref, low_ref, base_ref, up_query_ref, up_value_ref, suffix_ref = refs[:8]
-    sources, (query_ref, largest_ref, weighted_ref, total_ref, page_ref) = refs[8:-5], refs[-5:]
+    sources, (query_ref, largest_ref, weighted_ref, total_ref, page_ref, semaphores) = refs[8:-6], refs[-6:]
     rows = base_ref.shape[0]
+    flags = read_flags(owner_of(places_ref, tenant_ref))
+    copies = [
+        fetch_read(
+            flags,
+            page_ref.at[begin:end],
+            sources[part * routes : (part + 1) * routes],
+            semaphores.at[part],
+        )
+        for part, (begin, end) in enumerate(cuts)
+    ]
     choice = choice_ref[0]
     low = low_ref[...].astype(jnp.bfloat16)
     update = lax.dot_general(low[:rank], up_query_ref[choice], TN, preferred_element_type=jnp.float32)
     query_ref[...] = (base_ref[...].astype(jnp.float32) + update).astype(jnp.bfloat16)
     delta = lax.dot_general(low[rank:], up_value_ref[choice], TN, preferred_element_type=jnp.float32)
-    flags = read_flags(owner_of(places_ref, tenant_ref))
-    for part, (begin, end) in enumerate(cuts):
-        copy_read(flags, page_ref, slice(begin, end), sources[part * routes : (part + 1) * routes])
     row = lax.broadcasted_iota(jnp.int32, (rows, rows), 0)
     column = lax.broadcasted_iota(jnp.int32, (rows, rows), 1)
     seen = column <= row
+    for copy in copies:
+        copy.wait()
     for head in range(heads):
         start = 2 * width * head
         base_value = suffix_ref[:, start + width : start + 2 * width].astype(jnp.float32)
@@ -101,10 +112,10 @@
 def last_kernel(shape, read_flags, *refs):
     heads, group, width, rank, scale = shape
     places_ref, tenant_ref, blocks_ref, query_ref, largest_ref, weighted_ref, total_ref = refs[:7]
-    sources, (out_ref, page_ref) = refs[7:-2], refs[-2:]
+    sources, (out_ref, page_ref, semaphore) = refs[7:-3], refs[-3:]
     rows = query_ref.shape[0]
     flags = read_flags(owner_of(places_ref, tenant_ref))
-    copy_read(flags, page_ref, slice(0, page_ref.shape[0]), sources)
+    fetch_read(flags, page_ref, sources, semaphore).wait()
     live = lax.broadcasted_iota(jnp.int32, (rows, width), 0) < blocks_ref[0] * STRETCH
     for head in range(heads):
         start = 2 * width * head
@@ -127,7 +138,16 @@
     return pltpu.with_memory_space_constraint(array, pltpu.VMEM)
 
 
+def in_hbm(array):
+    return pltpu.with_memory_space_constraint(array, pltpu.HBM)
+
+
+def tied(values, others):
+    return lax.optimization_barrier((values, others))[0]
+
+
 WHOLE = pl.BlockSpec(memory_space=pltpu.VMEM)
+FAR_AWAY = pl.BlockSpec(memory_space=pltpu.HBM)
 SCALARS = pl.BlockSpec(memory_space=pltpu.SMEM)
 
 
@@ -146,13 +166,16 @@
     return pl.pallas_call(
         functools.partial(first_kernel, shape, read_flags, cuts, len(parts[0])),
         out_shape=(pltpu.VMEM((rows, columns), jnp.bfloat16), state, state, state),
-        in_specs=[SCALARS] * 3 + [WHOLE] * (5 + len(sources)),
+        in_specs=[SCALARS] * 3 + [WHOLE] * 5 + [FAR_AWAY] * len(sources),
         out_specs=(WHOLE,) * 4,
-        scratch_shapes=[pltpu.VMEM((sum(depths), sources[0].shape[1]), jnp.bfloat16)],
+        scratch_shapes=[
+            pltpu.VMEM((sum(depths), sources[0].shape[1]), jnp.bfloat16),
+            pltpu.SemaphoreType.DMA((len(parts),)),
+        ],
         compiler_params=pltpu.CompilerParams(vmem_limit_bytes=VMEM_BYTES),
         cost_estimate=cost(rows, columns, sum(depths) + rows),
         name="attend_first",
-    )(*scalars, *inputs, *sources)
+    )(*scalars, *map(in_hbm, inputs), *map(in_hbm, sources))
 
 
 def attend_last(shape, read_flags, scalars, states, sources):
@@ -160,13 +183,13 @@
     return pl.pallas_call(
         functools.partial(last_kernel, shape, read_flags),
         out_shape=jax.ShapeDtypeStruct((rows, columns), jnp.bfloat16),
-        in_specs=[SCALARS] * 3 + [WHOLE] * (4 + len(sources)),
+        in_specs=[SCALARS] * 3 + [WHOLE] * 4 + [FAR_AWAY] * len(sources),
         out_specs=WHOLE,
-        scratch_shapes=[pltpu.VMEM(sources[0].shape, jnp.bfloat16)],
+        scratch_shapes=[pltpu.VMEM(sources[0].shape, jnp.bfloat16), pltpu.SemaphoreType.DMA],
         compiler_params=pltpu.CompilerParams(vmem_limit_bytes=VMEM_BYTES),
         cost_estimate=cost(rows, columns, sources[0].shape[0]),
         name="attend_last",
-    )(*scalars, *map(in_vmem, states), *sources)
+    )(*scalars, *map(in_vmem, states), *map(in_hbm, sources))
 
 
 def wish(places, tenant, columns):
@@ -199,17 +222,24 @@
 def line_attention(shape, page, places, tenant, blocks, low_of, inputs):
     count = len(PARTS)
     unit = page.shape[0] // sum(PARTS)
-    page = page.reshape(page.shape[0], -1)
-    own = [page[unit * sum(PARTS[:k]) : unit * sum(PARTS[: k + 1])] for k in range(count)]
-    wished = wish(places, tenant, page.shape[1])
+    own = [
+        page[unit * sum(PARTS[:k]) : unit * sum(PARTS[: k + 1])].reshape(unit * PARTS[k], -1)
+        for k in range(count)
+    ]
+    wished = wish(places, tenant, own[0].shape[1])
     wish_middle = moved(wished, MIDDLE)
     wish_far = moved(wished, TO_INSIDE)
-    edge = [moved(own[k], EDGES) for k in range(count)]
+    edge, middle, far = [moved(own[0], EDGES)], [], []
     low = low_of()
-    middle, far = [], []
     for k in range(count):
-        middle.append(moved(jnp.where(wish_middle > 0, edge[k], own[k]), MIDDLE))
-        far.append(moved(jnp.where(wish_far > 0, edge[k], own[k]), FAR))
+        if k + 1 < count:
+            before = (wish_middle, wish_far, edge[0]) if k == 0 else (edge[k - 1], low)
+            edge.append(moved(tied(own[k + 1], before), EDGES))
+        held, mine = edge[k], own[k]
+        if k >= 2:
+            held, mine = tied((held, mine), (middle[k - 2], far[k - 2]))
+        middle.append(moved(jnp.where(wish_middle > 0, held, mine), MIDDLE))
+        far.append(moved(jnp.where(wish_far > 0, held, mine), FAR))
     sources = list(zip(own, edge, middle, far))
     states = attend_first(
         shape, line_flags, (places, tenant, inputs[0]), (low, *inputs[1:]), sources[:-1]

time: 99.1 us -> 78.8 us (0.80)
  waiting for transfers between devices: 43.6 us -> 28.5 us
  local copies, waits for them, and re-layouts: 12.4 us -> 5.3 us
  starting transfers between devices: 21 us -> 22.9 us
  Pallas kernels: 14.2 us -> 16 us
  other arithmetic: 2.82 us -> 1.69 us
    ppermute x14, waiting for transfers between devices: 41.2 us -> 28.5 us  [moved(): return lax.ppermute(chunk, 'replica', pairs)]
    unnamed x39 -> x41, local copies, waits for them, and re-layouts: 10.2 us -> 3.32 us
    ppermute x2, waiting for transfers between devices: 2.43 us -> 0.01 us  [swap_sum(): lax.ppermute(value, axis, [(i, i ^ step) for i in range(size)])]
    ppermute x14, starting transfers between devices: 19.4 us -> 21.3 us  [moved(): return lax.ppermute(chunk, 'replica', pairs)]
    select_n x3 -> x4, other arithmetic: 1.99 us -> 1.01 us  [line_attention(): far.append(moved(jnp.where(wish_far > 0, held, mine), FAR))]
  transfers between devices with their start and end apart: 16 -> 16, of which waited for: 4 -> 5; matrix products, arithmetic and copies ran while one was open for 7% -> 9% of each run, Pallas kernels for 10% -> 13%
where the time goes in v2:
time: 78.8 us; the launch traced here: 78.3 us
  waiting for transfers between devices  28.5 us (36%)
  starting transfers between devices  22.9 us (29%)
  Pallas kernels  16 us (20%)
  local copies, waits for them, and re-layouts  5.3 us (7%)
  between operations  2.65 us (3%)
  other arithmetic  1.69 us (2%)
  matrix products  1.32 us (2%)
    ppermute x14, waiting for transfers between devices, moved(): return lax.ppermute(chunk, 'replica', pairs)  28.5 us
    ppermute x14, starting transfers between devices, moved(): return lax.ppermute(chunk, 'replica', pairs)  21.3 us
    pallas_call x1, Pallas kernels, attend_first(): pl.pallas_call(functools.partial(first_kernel, shape, read_flags, cuts, l...  10.2 us
    pallas_call x1, Pallas kernels, attend_last(): pl.pallas_call(functools.partial(last_kernel, shape, read_flags), out_sha...  4.54 us
    unnamed x41, local copies, waits for them, and re-layouts  3.32 us
    ppermute x2, starting transfers between devices, swap_sum(): lax.ppermute(value, axis, [(i, i ^ step) for i in range(size)])  1.63 us
  transfers between devices with their start and end apart: 16, of which 5 were waited for; matrix products, arithmetic and copies ran while one was open for 9% of the time, Pallas kernels for 13%

profile of v2, /device:TPU:0, one launch (start us, length us, event | category | flops | bytes accessed | tf_op | source)
XLA Modules:
  0.0 78.3 jit_solution(10119580793781168653)
XLA Ops:
  0.8 1.3 %wish.1 = f32[1,512]{1,0:T(1,128)} custom-call(s32[4]{0:T(128)} %refs_0_.3, s32[1]{0:T(128)S(6)} %copy.17.tenant_ref.refs_1_), custom_call_target="tpu_custom_call" | custom-call | tf_op jit(solution)/shard_map/wish/pallas_call | solution.py:196
  2.1 5.9 %collective-permute-start.5 = (f32[1,512]{1,0:T(1,128)}, f32[1,512]{1,0:T(1,128)S(1)}, u32[]{:S(2)}, u32[]{:S(2)}) collective-permute-start(f32[1,512]{1,0:T(1,128)} %wish.1), channel_id=1, source_target_pairs={{12,4},{0,8},{13,5},{1,9},{14,6},{2,10},{15,7},{3,11},{28,20},{16,... | collective-permute-start | bytes 6152 | tf_op jit(solution)/shard_map/ppermute | solution.py:211
  9.3 1.3 %fusion = f32[32,256]{1,0:T(8,128)S(1)} fusion(bf16[256,2048]{1,0:T(8,128)(2,1)S(1)} %copy-done, bf16[2,32,2048]{2,1,0:T(8,128)(2,1)} %param.15, s32[]{:T(128)S(6)} %select_n.31), kind=kOutput, calls=%fused_computation.6 | convolution fusion | flops 33554432 | bytes 1212420 | tf_op jit(solution)/shard_map/dot_general | solution.py:289
  10.7 1.0 %slice.16 = bf16[1,128,2,256]{3,2,1,0:T(2,128)(2,1)S(1)} slice(bf16[1,1024,2,256]{3,2,1,0:T(2,128)(2,1)} %param.14), slice={[0:1], [0:128], [0:2], [0:256]} | slice | bytes 262144 | tf_op jit(solution)/shard_map/slice | solution.py:226
  11.8 1.3 %collective-permute-start.2 = (bf16[128,512]{1,0:T(8,128)(2,1)S(1)}, bf16[128,512]{1,0:T(8,128)(2,1)S(1)}, u32[]{:S(2)}, u32[]{:S(2)}) collective-permute-start(bf16[128,512]{1,0:T(8,128)(2,1)S(1)} %bitcast.35), channel_id=1, source_target_pairs={{0,4},{4,0},{8,12},{12,8},{1,5},{5,1},{9,13},{13,9},{2,6},{6,2},{1... | collective-permute-start | bytes 393224 | tf_op jit(solution)/shard_map/ppermute | solution.py:211
  13.7 1.6 %collective-permute-start.1 = (f32[32,256]{1,0:T(8,128)S(1)}, f32[32,256]{1,0:T(8,128)S(1)}, u32[]{:S(2)}, u32[]{:S(2)}) collective-permute-start(f32[32,256]{1,0:T(8,128)S(1)} %add.11), channel_id=1, source_target_pairs={{0,2},{1,3},{2,0},{3,1},{4,6},{5,7},{6,4},{7,5},{8,10},{9,11},{10,... | collective-permute-start | bytes 98312 | tf_op jit(solution)/shard_map/ppermute | solution.py:24
  15.2 2.5 %collective-permute-done.2.refs_9_ = bf16[128,512]{1,0:T(8,128)(2,1)S(1)} collective-permute-done((bf16[128,512]{1,0:T(8,128)(2,1)S(1)}, bf16[128,512]{1,0:T(8,128)(2,1)S(1)}, u32[]{:S(2)}, u32[]{:S(2)}) %collective-permute-start.2) | collective-permute-done | bytes 131104 | tf_op jit(solution)/shard_map/ppermute | solution.py:211
  17.7 1.2 %collective-permute-start.7 = (bf16[256,512]{1,0:T(8,128)(2,1)S(1)}, bf16[256,512]{1,0:T(8,128)(2,1)S(1)}, u32[]{:S(2)}, u32[]{:S(2)}) collective-permute-start(bf16[256,512]{1,0:T(8,128)(2,1)S(1)} %bitcast.29), channel_id=1, source_target_pairs={{0,4},{4,0},{8,12},{12,8},{1,5},{5,1},{9,13},{13,9},{2,6},{6,2},{1... | collective-permute-start | bytes 786440 | tf_op jit(solution)/shard_map/ppermute | solution.py:211
  19.6 0.8 %collective-permute-start.10 = (bf16[384,512]{1,0:T(8,128)(2,1)S(1)}, bf16[384,512]{1,0:T(8,128)(2,1)S(1)}, u32[]{:S(2)}, u32[]{:S(2)}) collective-permute-start(bf16[384,512]{1,0:T(8,128)(2,1)S(1)} %bitcast.26), channel_id=1, source_target_pairs={{0,4},{4,0},{8,12},{12,8},{1,5},{5,1},{9,13},{13,9},{2,6},{6,2},{1... | collective-permute-start | bytes 1179656 | tf_op jit(solution)/shard_map/ppermute | solution.py:211
  21.1 1.3 %collective-permute-start.6 = (bf16[128,512]{1,0:T(8,128)(2,1)S(1)}, bf16[128,512]{1,0:T(8,128)(2,1)S(1)}, u32[]{:S(2)}, u32[]{:S(2)}) collective-permute-start(bf16[128,512]{1,0:T(8,128)(2,1)S(1)} %get-tuple-element.35), channel_id=1, source_target_pairs={{4,12},{8,0},{5,13},{9,1},{6,14},{10,2},{7,15},{11,3},{20,28},{24,... | collective-permute-start | bytes 393224 | tf_op jit(solution)/shard_map/ppermute | solution.py:211
  22.4 5.8 %collective-permute-done.7.refs_13_ = bf16[256,512]{1,0:T(8,128)(2,1)S(1)} collective-permute-done((bf16[256,512]{1,0:T(8,128)(2,1)S(1)}, bf16[256,512]{1,0:T(8,128)(2,1)S(1)}, u32[]{:S(2)}, u32[]{:S(2)}) %collective-permute-start.7) | collective-permute-done | bytes 262176 | tf_op jit(solution)/shard_map/ppermute | solution.py:211
  29.0 1.3 %collective-permute-start.9 = (bf16[256,512]{1,0:T(8,128)(2,1)S(1)}, bf16[256,512]{1,0:T(8,128)(2,1)S(1)}, u32[]{:S(2)}, u32[]{:S(2)}) collective-permute-start(bf16[256,512]{1,0:T(8,128)(2,1)S(1)} %get-tuple-element.33), channel_id=1, source_target_pairs={{4,12},{8,0},{5,13},{9,1},{6,14},{10,2},{7,15},{11,3},{20,28},{24,... | collective-permute-start | bytes 786440 | tf_op jit(solution)/shard_map/ppermute | solution.py:211
  30.3 2.6 %collective-permute-start.13 = (bf16[256,512]{1,0:T(8,128)(2,1)S(1)}, bf16[256,512]{1,0:T(8,128)(2,1)S(1)}, u32[]{:S(2)}, u32[]{:S(2)}) collective-permute-start(bf16[256,512]{1,0:T(8,128)(2,1)S(1)} %bitcast.22), channel_id=1, source_target_pairs={{0,4},{4,0},{8,12},{12,8},{1,5},{5,1},{9,13},{13,9},{2,6},{6,2},{1... | collective-permute-start | bytes 786440 | tf_op jit(solution)/shard_map/ppermute | solution.py:211
  33.6 10.2 %collective-permute-done.10.refs_17_ = bf16[384,512]{1,0:T(8,128)(2,1)S(1)} collective-permute-done((bf16[384,512]{1,0:T(8,128)(2,1)S(1)}, bf16[384,512]{1,0:T(8,128)(2,1)S(1)}, u32[]{:S(2)}, u32[]{:S(2)}) %collective-permute-start.10) | collective-permute-done | bytes 393248 | tf_op jit(solution)/shard_map/ppermute | solution.py:211
  43.9 1.4 %collective-permute-start.11 = (bf16[384,512]{1,0:T(8,128)(2,1)S(1)}, bf16[384,512]{1,0:T(8,128)(2,1)}, u32[]{:S(2)}, u32[]{:S(2)}) collective-permute-start(bf16[384,512]{1,0:T(8,128)(2,1)S(1)} %get-tuple-element.30), channel_id=1, source_target_pairs={{4,8},{8,4},{5,9},{9,5},{6,10},{10,6},{7,11},{11,7},{20,24},{24,20... | collective-permute-start | bytes 1179656 | tf_op jit(solution)/shard_map/ppermute | solution.py:211
  45.3 1.3 %collective-permute-start.12 = (bf16[384,512]{1,0:T(8,128)(2,1)S(1)}, bf16[384,512]{1,0:T(8,128)(2,1)}, u32[]{:S(2)}, u32[]{:S(2)}) collective-permute-start(bf16[384,512]{1,0:T(8,128)(2,1)S(1)} %get-tuple-element.29), channel_id=1, source_target_pairs={{4,12},{8,0},{5,13},{9,1},{6,14},{10,2},{7,15},{11,3},{20,28},{24,... | collective-permute-start | bytes 1179656 | tf_op jit(solution)/shard_map/ppermute | solution.py:211
  46.6 5.7 %collective-permute-done.13.refs_8_ = bf16[256,512]{1,0:T(8,128)(2,1)S(1)} collective-permute-done((bf16[256,512]{1,0:T(8,128)(2,1)S(1)}, bf16[256,512]{1,0:T(8,128)(2,1)S(1)}, u32[]{:S(2)}, u32[]{:S(2)}) %collective-permute-start.13) | collective-permute-done | bytes 262176 | tf_op jit(solution)/shard_map/ppermute | solution.py:211
  52.4 0.9 %broadcast_select_fusion.2 = (bf16[256,512]{1,0:T(8,128)(2,1)}, bf16[256,512]{1,0:T(8,128)(2,1)}) fusion(bf16[256,512]{1,0:T(8,128)(2,1)S(1)} %collective-permute-done.13.refs_8_, bf16[256,512]{1,0:T(8,128)(2,1)S(1)} %bitcast.23, pred[512]{0:T(512)(128)(4,1)S(1)} %compare_reduce_fusion, pred[512]{0:T(512)(128)(4,1)S(1)} %compare_reduce_fusion.1), kind=kLoop, calls=%fused_computation.2 | loop fusion | flops 262144 | bytes 1049600 | tf_op jit(solution)/shard_map/jit(_where)/select_n | solution.py:242
  53.3 0.7 collective-permute-start.14
  54.0 1.5 %collective-permute-start.15 = (bf16[256,512]{1,0:T(8,128)(2,1)}, bf16[256,512]{1,0:T(8,128)(2,1)S(1)}, u32[]{:S(2)}, u32[]{:S(2)}) collective-permute-start(bf16[256,512]{1,0:T(8,128)(2,1)} %get-tuple-element.31), channel_id=1, source_target_pairs={{4,12},{8,0},{5,13},{9,1},{6,14},{10,2},{7,15},{11,3},{20,28},{24,... | collective-permute-start | bytes 786440 | tf_op jit(solution)/shard_map/ppermute | solution.py:211
  56.7 1.7 %copy.12 = bf16[32,8,2,256]{3,1,2,0:T(8,128)(2,1)} copy(bf16[32,8,2,256]{3,2,1,0:T(2,128)(2,1)} %bitcast.38) | data formatting | bytes 524288
  58.4 4.2 %collective-permute-done.12.refs_19_ = bf16[384,512]{1,0:T(8,128)(2,1)} collective-permute-done((bf16[384,512]{1,0:T(8,128)(2,1)S(1)}, bf16[384,512]{1,0:T(8,128)(2,1)}, u32[]{:S(2)}, u32[]{:S(2)}) %collective-permute-start.12) | collective-permute-done | bytes 393248 | tf_op jit(solution)/shard_map/ppermute | solution.py:211
  62.6 10.2 %attend_first.1 = (bf16[256,2048]{1,0:T(8,128)(2,1)S(1)}, f32[256,2048]{1,0:T(8,128)S(1)}, f32[256,2048]{1,0:T(8,128)S(1)}, f32[256,2048]{1,0:T(8,128)S(1)}) custom-call(s32[4]{0:T(128)S(1)} %copy-done.1, s32[1]{0:T(128)S(6)} %copy.17.tenant_ref.refs_1_, s32[1]{0:T(128)} %copy.19.refs_2_, f32[32,256]{1,0:T(8,128)} %add.12.refs_3_, ...), custom_call_target="tpu_custom_call" | custom-call | flops 2147483648 | bytes 2097152 | tf_op jit(solution)/shard_map/attend_first/pallas_call | solution.py:166
  73.6 4.5 %attend_last.1 = bf16[256,2048]{1,0:T(8,128)(2,1)} custom-call(s32[4]{0:T(128)S(1)} %copy-done.1, s32[1]{0:T(128)S(6)} %copy.17.tenant_ref.refs_1_, s32[1]{0:T(128)S(6)} %copy.18.refs_2_, bf16[256,2048]{1,0:T(8,128)(2,1)S(1)} %get-tuple-element.20.refs_3_, f32[256,2048]{1,0:T(8,128)S(1)} %get-tuple-element.21.refs_4_, ...), custom_call_target="tpu_custom_call" | custom-call | flops 536870912 | bytes 2097152 | tf_op jit(solution)/shard_map/attend_last/pallas_call | solution.py:183
  (66 shorter events, 5.5 us)
Async XLA Ops:
  2.1 11.5 %collective-permute-start.5 = (f32[1,512]{1,0:T(1,128)}, f32[1,512]{1,0:T(1,128)S(1)}, u32[]{:S(2)}, u32[]{:S(2)}) collective-permute-start(f32[1,512]{1,0:T(1,128)} %wish.1), channel_id=1, source_target_pairs={{12,4},{0,8},{13,5},{1,9},{14,6},{2,10},{15,7},{3,11},{28,20},{16,... | collective-permute-start | bytes 6152 | tf_op jit(solution)/shard_map/ppermute | solution.py:211
  8.0 7.2 %collective-permute-start.3 = (f32[1,512]{1,0:T(1,128)}, f32[1,512]{1,0:T(1,128)S(1)}, u32[]{:S(2)}, u32[]{:S(2)}) collective-permute-start(f32[1,512]{1,0:T(1,128)} %wish.1), channel_id=1, source_target_pairs={{4,8},{8,4},{5,9},{9,5},{6,10},{10,6},{7,11},{11,7},{20,24},{24,20... | collective-permute-start | bytes 6152 | tf_op jit(solution)/shard_map/ppermute | solution.py:211
  10.7 3.0 %collective-permute-start = (f32[32,256]{1,0:T(8,128)S(1)}, f32[32,256]{1,0:T(8,128)S(1)}, u32[]{:S(2)}, u32[]{:S(2)}) collective-permute-start(f32[32,256]{1,0:T(8,128)S(1)} %fusion), channel_id=1, source_target_pairs={{0,1},{1,0},{2,3},{3,2},{4,5},{5,4},{6,7},{7,6},{8,9},{9,8},{10,11... | collective-permute-start | bytes 98312 | tf_op jit(solution)/shard_map/ppermute | solution.py:24
  11.8 6.0 %collective-permute-start.2 = (bf16[128,512]{1,0:T(8,128)(2,1)S(1)}, bf16[128,512]{1,0:T(8,128)(2,1)S(1)}, u32[]{:S(2)}, u32[]{:S(2)}) collective-permute-start(bf16[128,512]{1,0:T(8,128)(2,1)S(1)} %bitcast.35), channel_id=1, source_target_pairs={{0,4},{4,0},{8,12},{12,8},{1,5},{5,1},{9,13},{13,9},{2,6},{6,2},{1... | collective-permute-start | bytes 393224 | tf_op jit(solution)/shard_map/ppermute | solution.py:211
  13.5 30.4 %copy-start.6 = (bf16[32,8,2,256]{3,1,2,0:T(8,128)(2,1)}, bf16[32,8,2,256]{3,1,2,0:T(8,128)(2,1)S(1)}, u32[]{:S(2)}) copy-start(bf16[32,8,2,256]{3,1,2,0:T(8,128)(2,1)S(1)} %copy.14) | copy-start | bytes 786436
  13.5 39.7 %copy-start.4 = (bf16[48,8,2,256]{3,1,2,0:T(8,128)(2,1)}, bf16[48,8,2,256]{3,1,2,0:T(8,128)(2,1)S(1)}, u32[]{:S(2)}) copy-start(bf16[48,8,2,256]{3,1,2,0:T(8,128)(2,1)S(1)} %copy.15) | copy-start | bytes 1179652
  13.6 39.7 %copy-start.2 = (bf16[32,8,2,256]{3,1,2,0:T(8,128)(2,1)}, bf16[32,8,2,256]{3,1,2,0:T(8,128)(2,1)S(1)}, u32[]{:S(2)}) copy-start(bf16[32,8,2,256]{3,1,2,0:T(8,128)(2,1)S(1)} %copy.16) | copy-start | bytes 786436
  13.7 5.3 %collective-permute-start.1 = (f32[32,256]{1,0:T(8,128)S(1)}, f32[32,256]{1,0:T(8,128)S(1)}, u32[]{:S(2)}, u32[]{:S(2)}) collective-permute-start(f32[32,256]{1,0:T(8,128)S(1)} %add.11), channel_id=1, source_target_pairs={{0,2},{1,3},{2,0},{3,1},{4,6},{5,7},{6,4},{7,5},{8,10},{9,11},{10,... | collective-permute-start | bytes 98312 | tf_op jit(solution)/shard_map/ppermute | solution.py:24
  17.7 35.5 %copy-start.12 = (bf16[128,512]{1,0:T(8,128)(2,1)}, bf16[128,512]{1,0:T(8,128)(2,1)S(1)}, u32[]{:S(2)}) copy-start(bf16[128,512]{1,0:T(8,128)(2,1)S(1)} %collective-permute-done.2.refs_9_) | copy-start | bytes 393220
  17.7 10.5 %collective-permute-start.7 = (bf16[256,512]{1,0:T(8,128)(2,1)S(1)}, bf16[256,512]{1,0:T(8,128)(2,1)S(1)}, u32[]{:S(2)}, u32[]{:S(2)}) collective-permute-start(bf16[256,512]{1,0:T(8,128)(2,1)S(1)} %bitcast.29), channel_id=1, source_target_pairs={{0,4},{4,0},{8,12},{12,8},{1,5},{5,1},{9,13},{13,9},{2,6},{6,2},{1... | collective-permute-start | bytes 786440 | tf_op jit(solution)/shard_map/ppermute | solution.py:211
  19.6 36.5 %copy-start.13 = (bf16[2,16,2,128]{3,2,1,0:T(2,128)(2,1)S(1)}, bf16[2,16,2,128]{3,2,1,0:T(2,128)(2,1)}, u32[]{:S(2)}) copy-start(bf16[2,16,2,128]{3,2,1,0:T(2,128)(2,1)} %param.17) | copy-start | bytes 49156
  19.6 24.2 %collective-permute-start.10 = (bf16[384,512]{1,0:T(8,128)(2,1)S(1)}, bf16[384,512]{1,0:T(8,128)(2,1)S(1)}, u32[]{:S(2)}, u32[]{:S(2)}) collective-permute-start(bf16[384,512]{1,0:T(8,128)(2,1)S(1)} %bitcast.26), channel_id=1, source_target_pairs={{0,4},{4,0},{8,12},{12,8},{1,5},{5,1},{9,13},{13,9},{2,6},{6,2},{1... | collective-permute-start | bytes 1179656 | tf_op jit(solution)/shard_map/ppermute | solution.py:211
  20.5 9.8 %collective-permute-start.4 = (bf16[128,512]{1,0:T(8,128)(2,1)S(1)}, bf16[128,512]{1,0:T(8,128)(2,1)S(1)}, u32[]{:S(2)}, u32[]{:S(2)}) collective-permute-start(bf16[128,512]{1,0:T(8,128)(2,1)S(1)} %get-tuple-element.36), channel_id=1, source_target_pairs={{4,8},{8,4},{5,9},{9,5},{6,10},{10,6},{7,11},{11,7},{20,24},{24,20... | collective-permute-start | bytes 393224 | tf_op jit(solution)/shard_map/ppermute | solution.py:211
  21.1 41.5 %copy-start.1 = (s32[4]{0:T(128)S(1)}, s32[4]{0:T(128)}, u32[]{:S(2)}) copy-start(s32[4]{0:T(128)} %refs_0_.3) | copy-start | bytes 52
  21.1 11.8 %collective-permute-start.6 = (bf16[128,512]{1,0:T(8,128)(2,1)S(1)}, bf16[128,512]{1,0:T(8,128)(2,1)S(1)}, u32[]{:S(2)}, u32[]{:S(2)}) collective-permute-start(bf16[128,512]{1,0:T(8,128)(2,1)S(1)} %get-tuple-element.35), channel_id=1, source_target_pairs={{4,12},{8,0},{5,13},{9,1},{6,14},{10,2},{7,15},{11,3},{20,28},{24,... | collective-permute-start | bytes 393224 | tf_op jit(solution)/shard_map/ppermute | solution.py:211
  28.3 18.3 %collective-permute-start.8 = (bf16[256,512]{1,0:T(8,128)(2,1)S(1)}, bf16[256,512]{1,0:T(8,128)(2,1)S(1)}, u32[]{:S(2)}, u32[]{:S(2)}) collective-permute-start(bf16[256,512]{1,0:T(8,128)(2,1)S(1)} %get-tuple-element.34), channel_id=1, source_target_pairs={{4,8},{8,4},{5,9},{9,5},{6,10},{10,6},{7,11},{11,7},{20,24},{24,20... | collective-permute-start | bytes 786440 | tf_op jit(solution)/shard_map/ppermute | solution.py:211
  29.0 17.6 %collective-permute-start.9 = (bf16[256,512]{1,0:T(8,128)(2,1)S(1)}, bf16[256,512]{1,0:T(8,128)(2,1)S(1)}, u32[]{:S(2)}, u32[]{:S(2)}) collective-permute-start(bf16[256,512]{1,0:T(8,128)(2,1)S(1)} %get-tuple-element.33), channel_id=1, source_target_pairs={{4,12},{8,0},{5,13},{9,1},{6,14},{10,2},{7,15},{11,3},{20,28},{24,... | collective-permute-start | bytes 786440 | tf_op jit(solution)/shard_map/ppermute | solution.py:211
  30.3 22.1 %collective-permute-start.13 = (bf16[256,512]{1,0:T(8,128)(2,1)S(1)}, bf16[256,512]{1,0:T(8,128)(2,1)S(1)}, u32[]{:S(2)}, u32[]{:S(2)}) collective-permute-start(bf16[256,512]{1,0:T(8,128)(2,1)S(1)} %bitcast.22), channel_id=1, source_target_pairs={{0,4},{4,0},{8,12},{12,8},{1,5},{5,1},{9,13},{13,9},{2,6},{6,2},{1... | collective-permute-start | bytes 786440 | tf_op jit(solution)/shard_map/ppermute | solution.py:211
  43.8 18.8 %copy-start.8 = (bf16[384,512]{1,0:T(8,128)(2,1)}, bf16[384,512]{1,0:T(8,128)(2,1)S(1)}, u32[]{:S(2)}) copy-start(bf16[384,512]{1,0:T(8,128)(2,1)S(1)} %collective-permute-done.10.refs_17_) | copy-start | bytes 1179652
  43.9 14.5 %collective-permute-start.11 = (bf16[384,512]{1,0:T(8,128)(2,1)S(1)}, bf16[384,512]{1,0:T(8,128)(2,1)}, u32[]{:S(2)}, u32[]{:S(2)}) collective-permute-start(bf16[384,512]{1,0:T(8,128)(2,1)S(1)} %get-tuple-element.30), channel_id=1, source_target_pairs={{4,8},{8,4},{5,9},{9,5},{6,10},{10,6},{7,11},{11,7},{20,24},{24,20... | collective-permute-start | bytes 1179656 | tf_op jit(solution)/shard_map/ppermute | solution.py:211
  45.3 17.3 %collective-permute-start.12 = (bf16[384,512]{1,0:T(8,128)(2,1)S(1)}, bf16[384,512]{1,0:T(8,128)(2,1)}, u32[]{:S(2)}, u32[]{:S(2)}) collective-permute-start(bf16[384,512]{1,0:T(8,128)(2,1)S(1)} %get-tuple-element.29), channel_id=1, source_target_pairs={{4,12},{8,0},{5,13},{9,1},{6,14},{10,2},{7,15},{11,3},{20,28},{24,... | collective-permute-start | bytes 1179656 | tf_op jit(solution)/shard_map/ppermute | solution.py:211
  52.4 20.5 %copy-start.5 = (bf16[256,512]{1,0:T(8,128)(2,1)}, bf16[256,512]{1,0:T(8,128)(2,1)S(1)}, u32[]{:S(2)}) copy-start(bf16[256,512]{1,0:T(8,128)(2,1)S(1)} %collective-permute-done.13.refs_8_) | copy-start | bytes 786436
  53.3 19.6 %collective-permute-start.14 = (bf16[256,512]{1,0:T(8,128)(2,1)}, bf16[256,512]{1,0:T(8,128)(2,1)S(1)}, u32[]{:S(2)}, u32[]{:S(2)}) collective-permute-start(bf16[256,512]{1,0:T(8,128)(2,1)} %get-tuple-element.32), channel_id=1, source_target_pairs={{4,8},{8,4},{5,9},{9,5},{6,10},{10,6},{7,11},{11,7},{20,24},{24,20... | collective-permute-start | bytes 786440 | tf_op jit(solution)/shard_map/ppermute | solution.py:211
  54.0 18.9 %collective-permute-start.15 = (bf16[256,512]{1,0:T(8,128)(2,1)}, bf16[256,512]{1,0:T(8,128)(2,1)S(1)}, u32[]{:S(2)}, u32[]{:S(2)}) collective-permute-start(bf16[256,512]{1,0:T(8,128)(2,1)} %get-tuple-element.31), channel_id=1, source_target_pairs={{4,12},{8,0},{5,13},{9,1},{6,14},{10,2},{7,15},{11,3},{20,28},{24,... | collective-permute-start | bytes 786440 | tf_op jit(solution)/shard_map/ppermute | solution.py:211
  (11 other events, 66.0 us)

commit v3 on v2

--- a/solution.py
+++ b/solution.py
@@ -73,19 +73,18 @@
 
 def first_kernel(shape, read_flags, cuts, routes, *refs):
     heads, group, width, rank, scale = shape
-    places_ref, tenant_ref, choice_ref, low_ref, base_ref, up_query_ref, up_value_ref, suffix_ref = refs[:8]
-    sources, (query_ref, largest_ref, weighted_ref, total_ref, page_ref, semaphores) = refs[8:-6], refs[-6:]
+    owner_ref, choice_ref, low_ref, base_ref, up_query_ref, up_value_ref, suffix_ref = refs[:7]
+    sources, (query_ref, largest_ref, weighted_ref, total_ref, page_ref, semaphores) = refs[7:-6], refs[-6:]
     rows = base_ref.shape[0]
-    flags = read_flags(owner_of(places_ref, tenant_ref))
-    copies = [
-        fetch_read(
-            flags,
-            page_ref.at[begin:end],
-            sources[part * routes : (part + 1) * routes],
-            semaphores.at[part],
+    flags = read_flags(owner_ref[0])
+    copies = []
+    for part, (begin, end) in enumerate(cuts):
+        count = len(routes[part])
+        chosen = [flags[route] for route in routes[part]]
+        copies.append(
+            fetch_read(chosen, page_ref.at[begin:end], sources[:count], semaphores.at[part])
         )
-        for part, (begin, end) in enumerate(cuts)
-    ]
+        sources = sources[count:]
     choice = choice_ref[0]
     low = low_ref[...].astype(jnp.bfloat16)
     update = lax.dot_general(low[:rank], up_query_ref[choice], TN, preferred_element_type=jnp.float32)
@@ -109,13 +108,18 @@
             largest_ref[:, at], weighted_ref[:, at], total_ref[:, at] = state
 
 
-def last_kernel(shape, read_flags, *refs):
+def last_kernel(shape, read_flags, routes, *refs):
     heads, group, width, rank, scale = shape
-    places_ref, tenant_ref, blocks_ref, query_ref, largest_ref, weighted_ref, total_ref = refs[:7]
-    sources, (out_ref, page_ref, semaphore) = refs[7:-3], refs[-3:]
+    owner_ref, blocks_ref, query_ref, largest_ref, weighted_ref, total_ref = refs[:6]
+    sources, (out_ref, page_ref) = refs[6:-2], refs[-2:]
     rows = query_ref.shape[0]
-    flags = read_flags(owner_of(places_ref, tenant_ref))
-    fetch_read(flags, page_ref, sources, semaphore).wait()
+    flags = read_flags(owner_ref[0])
+    for route, source in zip(routes, sources):
+
+        @pl.when(flags[route])
+        def _():
+            page_ref[...] = source[...]
+
     live = lax.broadcasted_iota(jnp.int32, (rows, width), 0) < blocks_ref[0] * STRETCH
     for head in range(heads):
         start = 2 * width * head
@@ -128,7 +132,7 @@
             out_ref[:, at] = jnp.where(live, weighted / total, 0.0).astype(jnp.bfloat16)
 
 
-def wish_kernel(places_ref, tenant_ref, out_ref):
+def wish_kernel(places_ref, tenant_ref, after_ref, out_ref):
     other_end = jnp.where(lax.axis_index("replica") >= 2, 0, 3)
     wished = jnp.where(owner_of(places_ref, tenant_ref) == other_end, 1.0, 0.0)
     out_ref[...] = jnp.full(out_ref.shape, wished, jnp.float32)
@@ -159,14 +163,15 @@
 
 def attend_first(shape, read_flags, scalars, inputs, parts):
     rows, columns = inputs[1].shape
-    depths = [sources[0].shape[0] for sources in parts]
+    depths = [part[0][1].shape[0] for part in parts]
     cuts = [(sum(depths[:k]), sum(depths[: k + 1])) for k in range(len(depths))]
+    routes = [[route for route, _ in part] for part in parts]
+    sources = [source for part in parts for _, source in part]
     state = pltpu.VMEM((rows, columns), jnp.float32)
-    sources = [source for sources in parts for source in sources]
     return pl.pallas_call(
-        functools.partial(first_kernel, shape, read_flags, cuts, len(parts[0])),
+        functools.partial(first_kernel, shape, read_flags, cuts, routes),
         out_shape=(pltpu.VMEM((rows, columns), jnp.bfloat16), state, state, state),
-        in_specs=[SCALARS] * 3 + [WHOLE] * 5 + [FAR_AWAY] * len(sources),
+        in_specs=[SCALARS] * 2 + [WHOLE] * 5 + [FAR_AWAY] * len(sources),
         out_specs=(WHOLE,) * 4,
         scratch_shapes=[
             pltpu.VMEM((sum(depths), sources[0].shape[1]), jnp.bfloat16),
@@ -178,28 +183,29 @@
     )(*scalars, *map(in_hbm, inputs), *map(in_hbm, sources))
 
 
-def attend_last(shape, read_flags, scalars, states, sources):
+def attend_last(shape, read_flags, scalars, states, part):
     rows, columns = states[0].shape
+    routes, sources = zip(*part)
     return pl.pallas_call(
-        functools.partial(last_kernel, shape, read_flags),
+        functools.partial(last_kernel, shape, read_flags, routes),
         out_shape=jax.ShapeDtypeStruct((rows, columns), jnp.bfloat16),
-        in_specs=[SCALARS] * 3 + [WHOLE] * 4 + [FAR_AWAY] * len(sources),
+        in_specs=[SCALARS] * 2 + [WHOLE] * (4 + len(sources)),
         out_specs=WHOLE,
-        scratch_shapes=[pltpu.VMEM(sources[0].shape, jnp.bfloat16), pltpu.SemaphoreType.DMA],
+        scratch_shapes=[pltpu.VMEM(sources[0].shape, jnp.bfloat16)],
         compiler_params=pltpu.CompilerParams(vmem_limit_bytes=VMEM_BYTES),
         cost_estimate=cost(rows, columns, sources[0].shape[0]),
         name="attend_last",
-    )(*scalars, *map(in_vmem, states), *map(in_hbm, sources))
-
-
-def wish(places, tenant, columns):
+    )(*scalars, *map(in_vmem, states), *map(in_vmem, sources))
+
+
+def wish(places, tenant, after, columns):
     return pl.pallas_call(
         wish_kernel,
         out_shape=jax.ShapeDtypeStruct((1, columns), jnp.float32),
-        in_specs=[SCALARS] * 2,
+        in_specs=[SCALARS] * 2 + [pl.BlockSpec(memory_space=pl.ANY)],
         out_specs=WHOLE,
         name="wish",
-    )(places, tenant)
+    )(places, tenant, after)
 
 
 EDGES, MIDDLE, FAR = [(0, 1), (1, 0), (2, 3), (3, 2)], [(1, 2), (2, 1)], [(1, 3), (2, 0)]
@@ -226,25 +232,31 @@
         page[unit * sum(PARTS[:k]) : unit * sum(PARTS[: k + 1])].reshape(unit * PARTS[k], -1)
         for k in range(count)
     ]
-    wished = wish(places, tenant, own[0].shape[1])
+    edge, middle, far = [moved(own[0], EDGES)], [], []
+    wished = wish(places, tenant, own[0], own[0].shape[1])
     wish_middle = moved(wished, MIDDLE)
     wish_far = moved(wished, TO_INSIDE)
-    edge, middle, far = [moved(own[0], EDGES)], [], []
-    low = low_of()
+    low = None
     for k in range(count):
         if k + 1 < count:
-            before = (wish_middle, wish_far, edge[0]) if k == 0 else (edge[k - 1], low)
-            edge.append(moved(tied(own[k + 1], before), EDGES))
+            edge.append(moved(tied(own[k + 1], (edge[k], wished) if k == 0 else edge[k]), EDGES))
         held, mine = edge[k], own[k]
-        if k >= 2:
-            held, mine = tied((held, mine), (middle[k - 2], far[k - 2]))
+        if k == 1:
+            held, mine = tied((held, mine), edge[k])
+        if k == 2:
+            held, mine = tied((held, mine), (middle[0],))
+        if k >= 3:
+            held, mine = tied((held, mine), (middle[k - 2], far[k - 2], low))
         middle.append(moved(jnp.where(wish_middle > 0, held, mine), MIDDLE))
         far.append(moved(jnp.where(wish_far > 0, held, mine), FAR))
-    sources = list(zip(own, edge, middle, far))
+        if k == 1:
+            low = low_of((middle[0], far[0], edge[1]))
+    parts = [list(enumerate(routes)) for routes in zip(own, edge, middle, far)]
+    owner = lax.dynamic_slice(places, tied(tenant, edge[1]), (1,))
     states = attend_first(
-        shape, line_flags, (places, tenant, inputs[0]), (low, *inputs[1:]), sources[:-1]
-    )
-    return attend_last(shape, line_flags, (places, tenant, blocks), states, sources[-1])
+        shape, line_flags, (owner, inputs[0]), (low, *inputs[1:]), parts[:-1]
+    )
+    return attend_last(shape, line_flags, (owner, blocks), states, parts[-1])
 
 
 def ring_attention(shape, page, places, tenant, blocks, low_of, inputs):
@@ -258,11 +270,15 @@
     page = page.reshape(page.shape[0], -1)
     cut = page.shape[0] * 3 // 4
     shifts = [[(i, (i + by) % size) for i in range(size)] for by in range(1, READ_SPAN)]
-    parts = [[part] + [moved(part, pairs) for pairs in shifts] for part in (page[:cut], page[cut:])]
+    parts = [
+        list(enumerate([part] + [moved(part, pairs) for pairs in shifts]))
+        for part in (page[:cut], page[cut:])
+    ]
+    owner = lax.dynamic_slice(places, tenant, (1,))
     states = attend_first(
-        shape, read_flags, (places, tenant, inputs[0]), (low_of(), *inputs[1:]), parts[:1]
-    )
-    return attend_last(shape, read_flags, (places, tenant, blocks), states, parts[1])
+        shape, read_flags, (owner, inputs[0]), (low_of(page), *inputs[1:]), parts[:1]
+    )
+    return attend_last(shape, read_flags, (owner, blocks), states, parts[1])
 
 
 def on_device(
@@ -284,9 +300,10 @@
     adapters, rank = adapter_down.shape[0], adapter_down.shape[1] // 2
     shape = (heads, group, width, rank, math.log2(math.e) / math.sqrt(width))
 
-    def low_of():
+    def low_of(before):
+        hidden = tied(suffix_hidden, before)
         down = lax.dynamic_index_in_dim(adapter_down, request_adapter[0], 0, keepdims=False)
-        low = lax.dot_general(down, suffix_hidden, NT, preferred_element_type=jnp.float32)
+        low = lax.dot_general(down, hidden, NT, preferred_element_type=jnp.float32)
         return swap_sum(low, "tensor")
 
     inputs = (

time: 78.8 us -> 76.8 us (0.975)
  waiting for transfers between devices: 28.5 us -> 25.2 us
  other arithmetic: 1.69 us -> 3.78 us
  starting transfers between devices: 22.9 us -> 21.5 us
  local copies, waits for them, and re-layouts: 5.3 us -> 6.27 us
    ppermute x14, waiting for transfers between devices: 28.5 us -> 25.2 us  [moved(): return lax.ppermute(chunk, 'replica', pairs)]
    select_n x4, other arithmetic: 1.01 us -> 3.12 us  [line_attention(): far.append(moved(jnp.where(wish_far > 0, held, mine), FAR))]
    unnamed x41 -> x37, local copies, waits for them, and re-layouts: 3.32 us -> 1.9 us
    ppermute x14, starting transfers between devices: 21.3 us -> 19.9 us  [moved(): return lax.ppermute(chunk, 'replica', pairs)]
    dynamic_slice x0 -> x1, local copies, waits for them, and re-layouts: none -> 1.25 us  [line_attention(): owner = lax.dynamic_slice(places, tied(tenant, edge[1]), (1,))]
    slice x4, local copies, waits for them, and re-layouts: 1.36 us -> 2.5 us  [line_attention(): page[unit * sum(PARTS[:k]):unit * sum(PARTS[:k + 1])]]
  transfers between devices with their start and end apart: 16 -> 16, of which waited for: 5 -> 5; matrix products, arithmetic and copies ran while one was open for 9% -> 13% of each run, Pallas kernels for 13% -> 16%
where the time goes in v3:
time: 76.8 us; the launch traced here: 76.3 us
  waiting for transfers between devices  25.2 us (33%)
  starting transfers between devices  21.5 us (28%)
  Pallas kernels  15.8 us (21%)
  local copies, waits for them, and re-layouts  6.27 us (8%)
  other arithmetic  3.78 us (5%)
  between operations  2.37 us (3%)
  matrix products  1.32 us (2%)
    ppermute x14, waiting for transfers between devices, moved(): return lax.ppermute(chunk, 'replica', pairs)  25.2 us
    ppermute x14, starting transfers between devices, moved(): return lax.ppermute(chunk, 'replica', pairs)  19.9 us
    pallas_call x1, Pallas kernels, attend_first(): pl.pallas_call(functools.partial(first_kernel, shape, read_flags, cuts, r...  10.8 us
    pallas_call x1, Pallas kernels, attend_last(): pl.pallas_call(functools.partial(last_kernel, shape, read_flags, routes),...  3.68 us
    select_n x4, other arithmetic, line_attention(): far.append(moved(jnp.where(wish_far > 0, held, mine), FAR))  3.12 us
    slice x4, local copies, waits for them, and re-layouts, line_attention(): page[unit * sum(PARTS[:k]):unit * sum(PARTS[:k + 1])]  2.5 us
    unnamed x37, local copies, waits for them, and re-layouts  1.9 us
    ppermute x2, starting transfers between devices, swap_sum(): lax.ppermute(value, axis, [(i, i ^ step) for i in range(size)])  1.63 us
  transfers between devices with their start and end apart: 16, of which 5 were waited for; matrix products, arithmetic and copies ran while one was open for 13% of the time, Pallas kernels for 16%

profile of v3, /device:TPU:0, one launch (start us, length us, event | category | flops | bytes accessed | tf_op | source)
XLA Modules:
  0.0 76.3 jit_solution(5812793022880436959)
XLA Ops:
  0.0 1.1 %slice.17 = bf16[1,128,2,256]{3,2,1,0:T(2,128)(2,1)S(1)} slice(bf16[1,1024,2,256]{3,2,1,0:T(2,128)(2,1)} %param.14), slice={[0:1], [0:128], [0:2], [0:256]} | slice | bytes 262144 | tf_op jit(solution)/shard_map/slice | solution.py:232
  1.1 3.1 %collective-permute-start = (bf16[128,512]{1,0:T(8,128)(2,1)S(1)}, bf16[128,512]{1,0:T(8,128)(2,1)S(1)}, u32[]{:S(2)}, u32[]{:S(2)}) collective-permute-start(bf16[128,512]{1,0:T(8,128)(2,1)S(1)} %bitcast.33), channel_id=1, source_target_pairs={{0,4},{4,0},{8,12},{12,8},{1,5},{5,1},{9,13},{13,9},{2,6},{6,2},{1... | collective-permute-start | bytes 393224 | tf_op jit(solution)/shard_map/ppermute | solution.py:217
  4.9 1.3 %wish.1 = f32[1,512]{1,0:T(1,128)} custom-call(s32[4]{0:T(128)} %places_ref.1, s32[1]{0:T(128)} %copy.17.tenant_ref, bf16[128,512]{1,0:T(8,128)(2,1)} %bitcast.34), custom_call_target="tpu_custom_call" | custom-call | tf_op jit(solution)/shard_map/wish/pallas_call | solution.py:202
  6.2 4.5 %collective-permute-start.4 = (f32[1,512]{1,0:T(1,128)}, f32[1,512]{1,0:T(1,128)S(1)}, u32[]{:S(2)}, u32[]{:S(2)}) collective-permute-start(f32[1,512]{1,0:T(1,128)} %wish.1), channel_id=1, source_target_pairs={{12,4},{0,8},{13,5},{1,9},{14,6},{2,10},{15,7},{3,11},{28,20},{16,... | collective-permute-start | bytes 6152 | tf_op jit(solution)/shard_map/ppermute | solution.py:217
  11.3 1.4 %fusion.4 = (bf16[1,256,2,256]{3,2,1,0:T(2,128)(2,1)S(1)}, bf16[1,256,2,256]{3,2,1,0:T(2,128)(2,1)S(1)}) fusion(bf16[1,1024,2,256]{3,2,1,0:T(2,128)(2,1)} %param.14), kind=kLoop, calls=%fused_computation.14 | loop fusion | bytes 1048576 | tf_op jit(solution)/shard_map/slice | solution.py:232
  12.9 1.5 %collective-permute-start.1 = (bf16[256,512]{1,0:T(8,128)(2,1)S(1)}, bf16[256,512]{1,0:T(8,128)(2,1)S(1)}, u32[]{:S(2)}, u32[]{:S(2)}) collective-permute-start(bf16[256,512]{1,0:T(8,128)(2,1)S(1)} %bitcast.37), channel_id=1, source_target_pairs={{0,4},{4,0},{8,12},{12,8},{1,5},{5,1},{9,13},{13,9},{2,6},{6,2},{1... | collective-permute-start | bytes 786440 | tf_op jit(solution)/shard_map/ppermute | solution.py:217
  14.4 0.9 %broadcast_select_fusion.6 = (bf16[128,512]{1,0:T(8,128)(2,1)S(1)}, bf16[128,512]{1,0:T(8,128)(2,1)S(1)}) fusion(bf16[128,512]{1,0:T(8,128)(2,1)S(1)} %collective-permute-done.refs_8_, bf16[128,512]{1,0:T(8,128)(2,1)} %bitcast.35, pred[512]{0:T(512)(128)(4,1)S(1)} %compare_reduce_fusion, pred[512]{0:T(512)(128)(4,1)S(1)} %compare_reduce_fusion.1), kind=kLoop, calls=%fused_computation.9 | loop fusion | flops 131072 | bytes 525312 | tf_op jit(solution)/shard_map/jit(_where)/select_n | solution.py:251
  16.0 1.3 %collective-permute-start.5 = (bf16[128,512]{1,0:T(8,128)(2,1)S(1)}, bf16[128,512]{1,0:T(8,128)(2,1)S(1)}, u32[]{:S(2)}, u32[]{:S(2)}) collective-permute-start(bf16[128,512]{1,0:T(8,128)(2,1)S(1)} %get-tuple-element.43), channel_id=1, source_target_pairs={{4,12},{8,0},{5,13},{9,1},{6,14},{10,2},{7,15},{11,3},{20,28},{24,... | collective-permute-start | bytes 393224 | tf_op jit(solution)/shard_map/ppermute | solution.py:217
  18.1 6.3 %collective-permute-done.5.refs_10_ = bf16[128,512]{1,0:T(8,128)(2,1)S(1)} collective-permute-done((bf16[128,512]{1,0:T(8,128)(2,1)S(1)}, bf16[128,512]{1,0:T(8,128)(2,1)S(1)}, u32[]{:S(2)}, u32[]{:S(2)}) %collective-permute-start.5) | collective-permute-done | bytes 131104 | tf_op jit(solution)/shard_map/ppermute | solution.py:217
  24.6 1.3 %fusion = f32[32,256]{1,0:T(8,128)S(1)} fusion(bf16[256,2048]{1,0:T(8,128)(2,1)S(1)} %copy-done, bf16[2,32,2048]{2,1,0:T(8,128)(2,1)} %param.15, s32[]{:T(128)S(6)} %select_n.35), kind=kOutput, calls=%fused_computation.6 | convolution fusion | flops 33554432 | bytes 1212420 | tf_op jit(solution)/shard_map/dot_general | solution.py:306
  27.4 1.3 %collective-permute-start.9 = (bf16[256,512]{1,0:T(8,128)(2,1)S(1)}, bf16[256,512]{1,0:T(8,128)(2,1)S(1)}, u32[]{:S(2)}, u32[]{:S(2)}) collective-permute-start(bf16[256,512]{1,0:T(8,128)(2,1)S(1)} %get-tuple-element.41), channel_id=1, source_target_pairs={{4,12},{8,0},{5,13},{9,1},{6,14},{10,2},{7,15},{11,3},{20,28},{24,... | collective-permute-start | bytes 786440 | tf_op jit(solution)/shard_map/ppermute | solution.py:217
  28.7 1.6 %collective-permute-start.7 = (f32[32,256]{1,0:T(8,128)S(1)}, f32[32,256]{1,0:T(8,128)S(1)}, u32[]{:S(2)}, u32[]{:S(2)}) collective-permute-start(f32[32,256]{1,0:T(8,128)S(1)} %add.15), channel_id=1, source_target_pairs={{0,2},{1,3},{2,0},{3,1},{4,6},{5,7},{6,4},{7,5},{8,10},{9,11},{10,... | collective-permute-start | bytes 98312 | tf_op jit(solution)/shard_map/ppermute | solution.py:24
  30.2 3.1 %collective-permute-done.10.refs_16_ = bf16[384,512]{1,0:T(8,128)(2,1)S(1)} collective-permute-done((bf16[384,512]{1,0:T(8,128)(2,1)S(1)}, bf16[384,512]{1,0:T(8,128)(2,1)S(1)}, u32[]{:S(2)}, u32[]{:S(2)}) %collective-permute-start.10) | collective-permute-done | bytes 393248 | tf_op jit(solution)/shard_map/ppermute | solution.py:217
  33.3 1.5 %collective-permute-start.13 = (bf16[256,512]{1,0:T(8,128)(2,1)S(1)}, bf16[256,512]{1,0:T(8,128)(2,1)S(1)}, u32[]{:S(2)}, u32[]{:S(2)}) collective-permute-start(bf16[256,512]{1,0:T(8,128)(2,1)S(1)} %bitcast.26), channel_id=1, source_target_pairs={{0,4},{4,0},{8,12},{12,8},{1,5},{5,1},{9,13},{13,9},{2,6},{6,2},{1... | collective-permute-start | bytes 786440 | tf_op jit(solution)/shard_map/ppermute | solution.py:217
  35.6 1.4 %collective-permute-start.11 = (bf16[384,512]{1,0:T(8,128)(2,1)}, bf16[384,512]{1,0:T(8,128)(2,1)}, u32[]{:S(2)}, u32[]{:S(2)}) collective-permute-start(bf16[384,512]{1,0:T(8,128)(2,1)} %get-tuple-element.38), channel_id=1, source_target_pairs={{4,8},{8,4},{5,9},{9,5},{6,10},{10,6},{7,11},{11,7},{20,24},{24,20... | collective-permute-start | bytes 1179656 | tf_op jit(solution)/shard_map/ppermute | solution.py:217
  37.1 1.3 %collective-permute-start.12 = (bf16[384,512]{1,0:T(8,128)(2,1)S(1)}, bf16[384,512]{1,0:T(8,128)(2,1)}, u32[]{:S(2)}, u32[]{:S(2)}) collective-permute-start(bf16[384,512]{1,0:T(8,128)(2,1)S(1)} %get-tuple-element.37), channel_id=1, source_target_pairs={{4,12},{8,0},{5,13},{9,1},{6,14},{10,2},{7,15},{11,3},{20,28},{24,... | collective-permute-start | bytes 1179656 | tf_op jit(solution)/shard_map/ppermute | solution.py:217
  39.0 5.8 %collective-permute-done.9.refs_14_ = bf16[256,512]{1,0:T(8,128)(2,1)S(1)} collective-permute-done((bf16[256,512]{1,0:T(8,128)(2,1)S(1)}, bf16[256,512]{1,0:T(8,128)(2,1)S(1)}, u32[]{:S(2)}, u32[]{:S(2)}) %collective-permute-start.9) | collective-permute-done | bytes 262176 | tf_op jit(solution)/shard_map/ppermute | solution.py:217
  44.8 2.1 %collective-permute-done.13.refs_7_ = bf16[256,512]{1,0:T(8,128)(2,1)S(1)} collective-permute-done((bf16[256,512]{1,0:T(8,128)(2,1)S(1)}, bf16[256,512]{1,0:T(8,128)(2,1)S(1)}, u32[]{:S(2)}, u32[]{:S(2)}) %collective-permute-start.13) | collective-permute-done | bytes 262176 | tf_op jit(solution)/shard_map/ppermute | solution.py:217
  48.3 1.3 %collective-permute-start.15 = (bf16[256,512]{1,0:T(8,128)(2,1)S(1)}, bf16[256,512]{1,0:T(8,128)(2,1)S(1)}, u32[]{:S(2)}, u32[]{:S(2)}) collective-permute-start(bf16[256,512]{1,0:T(8,128)(2,1)S(1)} %get-tuple-element.39), channel_id=1, source_target_pairs={{4,12},{8,0},{5,13},{9,1},{6,14},{10,2},{7,15},{11,3},{20,28},{24,... | collective-permute-start | bytes 786440 | tf_op jit(solution)/shard_map/ppermute | solution.py:217
  49.6 1.2 %dynamic_slice.7.refs_0_ = s32[1]{0:T(128)} dynamic-slice(s32[4]{0:T(128)} %places_ref.1, s32[]{:T(128)S(6)} %select_n.34), dynamic_slice_sizes={1} | dynamic-slice | bytes 12 | tf_op jit(solution)/shard_map/dynamic_slice | solution.py:255
  52.1 1.7 %copy.14 = bf16[32,8,2,256]{3,1,2,0:T(8,128)(2,1)} copy(bf16[32,8,2,256]{3,2,1,0:T(2,128)(2,1)} %bitcast.43) | data formatting | bytes 524288
  53.8 7.9 %collective-permute-done.12.refs_18_ = bf16[384,512]{1,0:T(8,128)(2,1)} collective-permute-done((bf16[384,512]{1,0:T(8,128)(2,1)S(1)}, bf16[384,512]{1,0:T(8,128)(2,1)}, u32[]{:S(2)}, u32[]{:S(2)}) %collective-permute-start.12) | collective-permute-done | bytes 393248 | tf_op jit(solution)/shard_map/ppermute | solution.py:217
  61.7 10.8 %attend_first.1 = (bf16[256,2048]{1,0:T(8,128)(2,1)S(1)}, f32[256,2048]{1,0:T(8,128)S(1)}, f32[256,2048]{1,0:T(8,128)S(1)}, f32[256,2048]{1,0:T(8,128)S(1)}) custom-call(s32[1]{0:T(128)} %dynamic_slice.7.refs_0_, s32[1]{0:T(128)} %copy.19.refs_1_, f32[32,256]{1,0:T(8,128)} %add.16.refs_2_, bf16[256,2048]{1,0:T(8,128)(2,1)} %refs_3_.1, ...), custom_call_target="tpu_custom_call" | custom-call | flops 2147483648 | bytes 2097152 | tf_op jit(solution)/shard_map/attend_first/pallas_call | solution.py:171
  72.6 3.7 %attend_last.1 = bf16[256,2048]{1,0:T(8,128)(2,1)} custom-call(s32[1]{0:T(128)} %dynamic_slice.7.refs_0_, s32[1]{0:T(128)S(6)} %copy.18.refs_1_, bf16[256,2048]{1,0:T(8,128)(2,1)S(1)} %get-tuple-element.28.refs_2_, f32[256,2048]{1,0:T(8,128)S(1)} %get-tuple-element.29.refs_3_, f32[256,2048]{1,0:T(8,128)S(1)} %get-tuple-element.30.refs_4_, ...), custom_call_target="tpu_custom_call" | custom-call | flops 536870912 | bytes 2097152 | tf_op jit(solution)/shard_map/attend_last/pallas_call | solution.py:189
  (63 shorter events, 6.5 us)
Async XLA Ops:
  0.0 24.6 %copy-start = (bf16[256,2048]{1,0:T(8,128)(2,1)S(1)}, bf16[256,2048]{1,0:T(8,128)(2,1)}, u32[]{:S(2)}) copy-start(bf16[256,2048]{1,0:T(8,128)(2,1)} %param.11) | copy-start | bytes 3145732
  0.0 17.9 %slice-start = ((bf16[1,1024,2,256]{3,2,1,0:T(2,128)(2,1)}), bf16[1,384,2,256]{3,2,1,0:T(2,128)(2,1)S(1)}, s32[]{:S(2)}) async-start(bf16[1,1024,2,256]{3,2,1,0:T(2,128)(2,1)} %param.14), calls=%async_computation | async-start | bytes 786432 | tf_op jit(solution)/shard_map/slice | solution.py:232
  1.1 11.7 %collective-permute-start = (bf16[128,512]{1,0:T(8,128)(2,1)S(1)}, bf16[128,512]{1,0:T(8,128)(2,1)S(1)}, u32[]{:S(2)}, u32[]{:S(2)}) collective-permute-start(bf16[128,512]{1,0:T(8,128)(2,1)S(1)} %bitcast.33), channel_id=1, source_target_pairs={{0,4},{4,0},{8,12},{12,8},{1,5},{5,1},{9,13},{13,9},{2,6},{6,2},{1... | collective-permute-start | bytes 393224 | tf_op jit(solution)/shard_map/ppermute | solution.py:217
  6.2 6.6 %collective-permute-start.4 = (f32[1,512]{1,0:T(1,128)}, f32[1,512]{1,0:T(1,128)S(1)}, u32[]{:S(2)}, u32[]{:S(2)}) collective-permute-start(f32[1,512]{1,0:T(1,128)} %wish.1), channel_id=1, source_target_pairs={{12,4},{0,8},{13,5},{1,9},{14,6},{2,10},{15,7},{3,11},{28,20},{16,... | collective-permute-start | bytes 6152 | tf_op jit(solution)/shard_map/ppermute | solution.py:217
  10.6 2.2 %collective-permute-start.2 = (f32[1,512]{1,0:T(1,128)}, f32[1,512]{1,0:T(1,128)S(1)}, u32[]{:S(2)}, u32[]{:S(2)}) collective-permute-start(f32[1,512]{1,0:T(1,128)} %wish.1), channel_id=1, source_target_pairs={{4,8},{8,4},{5,9},{9,5},{6,10},{10,6},{7,11},{11,7},{20,24},{24,20... | collective-permute-start | bytes 6152 | tf_op jit(solution)/shard_map/ppermute | solution.py:217
  12.8 13.9 %copy-start.3 = (bf16[32,8,2,256]{3,1,2,0:T(8,128)(2,1)}, bf16[32,8,2,256]{3,1,2,0:T(8,128)(2,1)S(1)}, u32[]{:S(2)}) copy-start(bf16[32,8,2,256]{3,1,2,0:T(8,128)(2,1)S(1)} %copy.12) | copy-start | bytes 786436
  12.8 11.6 %copy-start.8 = (pred[512]{0:T(512)(128)(4,1)}, pred[512]{0:T(512)(128)(4,1)S(1)}, u32[]{:S(2)}) copy-start(pred[512]{0:T(512)(128)(4,1)S(1)} %compare_reduce_fusion) | copy-start | bytes 1540
  12.9 11.6 %collective-permute-start.1 = (bf16[256,512]{1,0:T(8,128)(2,1)S(1)}, bf16[256,512]{1,0:T(8,128)(2,1)S(1)}, u32[]{:S(2)}, u32[]{:S(2)}) collective-permute-start(bf16[256,512]{1,0:T(8,128)(2,1)S(1)} %bitcast.37), channel_id=1, source_target_pairs={{0,4},{4,0},{8,12},{12,8},{1,5},{5,1},{9,13},{13,9},{2,6},{6,2},{1... | collective-permute-start | bytes 786440 | tf_op jit(solution)/shard_map/ppermute | solution.py:217
  15.3 2.8 %collective-permute-start.3 = (bf16[128,512]{1,0:T(8,128)(2,1)S(1)}, bf16[128,512]{1,0:T(8,128)(2,1)S(1)}, u32[]{:S(2)}, u32[]{:S(2)}) collective-permute-start(bf16[128,512]{1,0:T(8,128)(2,1)S(1)} %get-tuple-element.44), channel_id=1, source_target_pairs={{4,8},{8,4},{5,9},{9,5},{6,10},{10,6},{7,11},{11,7},{20,24},{24,20... | collective-permute-start | bytes 393224 | tf_op jit(solution)/shard_map/ppermute | solution.py:217
  16.0 8.4 %collective-permute-start.5 = (bf16[128,512]{1,0:T(8,128)(2,1)S(1)}, bf16[128,512]{1,0:T(8,128)(2,1)S(1)}, u32[]{:S(2)}, u32[]{:S(2)}) collective-permute-start(bf16[128,512]{1,0:T(8,128)(2,1)S(1)} %get-tuple-element.43), channel_id=1, source_target_pairs={{4,12},{8,0},{5,13},{9,1},{6,14},{10,2},{7,15},{11,3},{20,28},{24,... | collective-permute-start | bytes 393224 | tf_op jit(solution)/shard_map/ppermute | solution.py:217
  18.0 17.6 %copy-start.1 = (bf16[48,8,2,256]{3,1,2,0:T(8,128)(2,1)}, bf16[48,8,2,256]{3,1,2,0:T(8,128)(2,1)S(1)}, u32[]{:S(2)}) copy-start(bf16[48,8,2,256]{3,1,2,0:T(8,128)(2,1)S(1)} %copy.15) | copy-start | bytes 1179652
  24.5 23.1 %copy-start.5 = (bf16[256,512]{1,0:T(8,128)(2,1)}, bf16[256,512]{1,0:T(8,128)(2,1)S(1)}, u32[]{:S(2)}) copy-start(bf16[256,512]{1,0:T(8,128)(2,1)S(1)} %collective-permute-done.1.refs_12_) | copy-start | bytes 786436
  24.5 8.9 %collective-permute-start.10 = (bf16[384,512]{1,0:T(8,128)(2,1)S(1)}, bf16[384,512]{1,0:T(8,128)(2,1)S(1)}, u32[]{:S(2)}, u32[]{:S(2)}) collective-permute-start(bf16[384,512]{1,0:T(8,128)(2,1)S(1)} %bitcast.30), channel_id=1, source_target_pairs={{0,4},{4,0},{8,12},{12,8},{1,5},{5,1},{9,13},{13,9},{2,6},{6,2},{1... | collective-permute-start | bytes 1179656 | tf_op jit(solution)/shard_map/ppermute | solution.py:217
  25.9 25.6 %copy-start.7 = (bf16[2,16,2,128]{3,2,1,0:T(2,128)(2,1)S(1)}, bf16[2,16,2,128]{3,2,1,0:T(2,128)(2,1)}, u32[]{:S(2)}) copy-start(bf16[2,16,2,128]{3,2,1,0:T(2,128)(2,1)} %param.17) | copy-start | bytes 49156
  25.9 2.7 %collective-permute-start.6 = (f32[32,256]{1,0:T(8,128)S(1)}, f32[32,256]{1,0:T(8,128)S(1)}, u32[]{:S(2)}, u32[]{:S(2)}) collective-permute-start(f32[32,256]{1,0:T(8,128)S(1)} %fusion), channel_id=1, source_target_pairs={{0,1},{1,0},{2,3},{3,2},{4,5},{5,4},{6,7},{7,6},{8,9},{9,8},{10,11... | collective-permute-start | bytes 98312 | tf_op jit(solution)/shard_map/ppermute | solution.py:24
  26.7 12.3 %collective-permute-start.8 = (bf16[256,512]{1,0:T(8,128)(2,1)S(1)}, bf16[256,512]{1,0:T(8,128)(2,1)S(1)}, u32[]{:S(2)}, u32[]{:S(2)}) collective-permute-start(bf16[256,512]{1,0:T(8,128)(2,1)S(1)} %get-tuple-element.42), channel_id=1, source_target_pairs={{4,8},{8,4},{5,9},{9,5},{6,10},{10,6},{7,11},{11,7},{20,24},{24,20... | collective-permute-start | bytes 786440 | tf_op jit(solution)/shard_map/ppermute | solution.py:217
  27.4 17.4 %collective-permute-start.9 = (bf16[256,512]{1,0:T(8,128)(2,1)S(1)}, bf16[256,512]{1,0:T(8,128)(2,1)S(1)}, u32[]{:S(2)}, u32[]{:S(2)}) collective-permute-start(bf16[256,512]{1,0:T(8,128)(2,1)S(1)} %get-tuple-element.41), channel_id=1, source_target_pairs={{4,12},{8,0},{5,13},{9,1},{6,14},{10,2},{7,15},{11,3},{20,28},{24,... | collective-permute-start | bytes 786440 | tf_op jit(solution)/shard_map/ppermute | solution.py:217
  28.7 8.4 %collective-permute-start.7 = (f32[32,256]{1,0:T(8,128)S(1)}, f32[32,256]{1,0:T(8,128)S(1)}, u32[]{:S(2)}, u32[]{:S(2)}) collective-permute-start(f32[32,256]{1,0:T(8,128)S(1)} %add.15), channel_id=1, source_target_pairs={{0,2},{1,3},{2,0},{3,1},{4,6},{5,7},{6,4},{7,5},{8,10},{9,11},{10,... | collective-permute-start | bytes 98312 | tf_op jit(solution)/shard_map/ppermute | solution.py:24
  33.3 28.4 %copy-start.4 = (bf16[384,512]{1,0:T(8,128)(2,1)}, bf16[384,512]{1,0:T(8,128)(2,1)S(1)}, u32[]{:S(2)}) copy-start(bf16[384,512]{1,0:T(8,128)(2,1)S(1)} %collective-permute-done.10.refs_16_) | copy-start | bytes 1179652
  33.3 13.5 %collective-permute-start.13 = (bf16[256,512]{1,0:T(8,128)(2,1)S(1)}, bf16[256,512]{1,0:T(8,128)(2,1)S(1)}, u32[]{:S(2)}, u32[]{:S(2)}) collective-permute-start(bf16[256,512]{1,0:T(8,128)(2,1)S(1)} %bitcast.26), channel_id=1, source_target_pairs={{0,4},{4,0},{8,12},{12,8},{1,5},{5,1},{9,13},{13,9},{2,6},{6,2},{1... | collective-permute-start | bytes 786440 | tf_op jit(solution)/shard_map/ppermute | solution.py:217
  35.6 18.2 %collective-permute-start.11 = (bf16[384,512]{1,0:T(8,128)(2,1)}, bf16[384,512]{1,0:T(8,128)(2,1)}, u32[]{:S(2)}, u32[]{:S(2)}) collective-permute-start(bf16[384,512]{1,0:T(8,128)(2,1)} %get-tuple-element.38), channel_id=1, source_target_pairs={{4,8},{8,4},{5,9},{9,5},{6,10},{10,6},{7,11},{11,7},{20,24},{24,20... | collective-permute-start | bytes 1179656 | tf_op jit(solution)/shard_map/ppermute | solution.py:217
  37.1 24.7 %collective-permute-start.12 = (bf16[384,512]{1,0:T(8,128)(2,1)S(1)}, bf16[384,512]{1,0:T(8,128)(2,1)}, u32[]{:S(2)}, u32[]{:S(2)}) collective-permute-start(bf16[384,512]{1,0:T(8,128)(2,1)S(1)} %get-tuple-element.37), channel_id=1, source_target_pairs={{4,12},{8,0},{5,13},{9,1},{6,14},{10,2},{7,15},{11,3},{20,28},{24,... | collective-permute-start | bytes 1179656 | tf_op jit(solution)/shard_map/ppermute | solution.py:217
  47.6 25.0 %collective-permute-start.14 = (bf16[256,512]{1,0:T(8,128)(2,1)}, bf16[256,512]{1,0:T(8,128)(2,1)S(1)}, u32[]{:S(2)}, u32[]{:S(2)}) collective-permute-start(bf16[256,512]{1,0:T(8,128)(2,1)} %get-tuple-element.40), channel_id=1, source_target_pairs={{4,8},{8,4},{5,9},{9,5},{6,10},{10,6},{7,11},{11,7},{20,24},{24,20... | collective-permute-start | bytes 786440 | tf_op jit(solution)/shard_map/ppermute | solution.py:217
  48.3 24.3 %collective-permute-start.15 = (bf16[256,512]{1,0:T(8,128)(2,1)S(1)}, bf16[256,512]{1,0:T(8,128)(2,1)S(1)}, u32[]{:S(2)}, u32[]{:S(2)}) collective-permute-start(bf16[256,512]{1,0:T(8,128)(2,1)S(1)} %get-tuple-element.39), channel_id=1, source_target_pairs={{4,12},{8,0},{5,13},{9,1},{6,14},{10,2},{7,15},{11,3},{20,28},{24,... | collective-permute-start | bytes 786440 | tf_op jit(solution)/shard_map/ppermute | solution.py:217
  (9 other events, 72.4 us)

commit v4 on v3

--- a/solution.py
+++ b/solution.py
@@ -210,7 +210,7 @@
 
 EDGES, MIDDLE, FAR = [(0, 1), (1, 0), (2, 3), (3, 2)], [(1, 2), (2, 1)], [(1, 3), (2, 0)]
 TO_INSIDE = [(3, 1), (0, 2)]
-PARTS = (1, 2, 3, 2)
+PARTS = (1, 3, 4)
 
 
 def moved(chunk, pairs):
@@ -238,19 +238,22 @@
     wish_far = moved(wished, TO_INSIDE)
     low = None
     for k in range(count):
-        if k + 1 < count:
-            edge.append(moved(tied(own[k + 1], (edge[k], wished) if k == 0 else edge[k]), EDGES))
+        if k == 0:
+            edge.append(moved(tied(own[1], (edge[0], (wish_middle, wish_far))), EDGES))
         held, mine = edge[k], own[k]
         if k == 1:
-            held, mine = tied((held, mine), edge[k])
+            held, mine = tied((held, mine), (middle[0], far[0]))
         if k == 2:
-            held, mine = tied((held, mine), (middle[0],))
+            held, mine = tied((held, mine), (middle[0], far[0]))
         if k >= 3:
             held, mine = tied((held, mine), (middle[k - 2], far[k - 2], low))
-        middle.append(moved(jnp.where(wish_middle > 0, held, mine), MIDDLE))
-        far.append(moved(jnp.where(wish_far > 0, held, mine), FAR))
+        inner, outer = jnp.where(wish_middle > 0, held, mine), jnp.where(wish_far > 0, held, mine)
+        if 1 <= k < count - 1:
+            edge.append(moved(tied(own[k + 1], (inner, outer)), EDGES))
+        middle.append(moved(inner, MIDDLE))
+        far.append(moved(outer, FAR))
         if k == 1:
-            low = low_of((middle[0], far[0], edge[1]))
+            low = low_of(middle[1])
     parts = [list(enumerate(routes)) for routes in zip(own, edge, middle, far)]
     owner = lax.dynamic_slice(places, tied(tenant, edge[1]), (1,))
     states = attend_first(

time: 76.8 us -> 74.5 us (0.970)
  starting transfers between devices: 21.5 us -> 18.1 us
  waiting for transfers between devices: 25.2 us -> 28.5 us
  local copies, waits for them, and re-layouts: 6.27 us -> 4.54 us
    ppermute x14 -> x11, starting transfers between devices: 19.9 us -> 16.5 us  [moved(): return lax.ppermute(chunk, 'replica', pairs)]
    ppermute x14 -> x11, waiting for transfers between devices: 25.2 us -> 27.3 us  [moved(): return lax.ppermute(chunk, 'replica', pairs)]
    pallas_call x1, Pallas kernels: 10.8 us -> 9.55 us  [attend_first(): pl.pallas_call(functools.partial(first_kernel, shape, read_flags, cuts, r...]
    pallas_call x1, Pallas kernels: 3.68 us -> 4.93 us  [attend_last(): pl.pallas_call(functools.partial(last_kernel, shape, read_flags, routes),...]
    ppermute x2, waiting for transfers between devices: 0.01 us -> 1.2 us  [swap_sum(): lax.ppermute(value, axis, [(i, i ^ step) for i in range(size)])]
    unnamed x37 -> x24, local copies, waits for them, and re-layouts: 1.9 us -> 0.95 us
    select_n x4 -> x3, other arithmetic: 3.12 us -> 2.97 us  [line_attention(): jnp.where(wish_far > 0, held, mine)]
  transfers between devices with their start and end apart: 16 -> 13, of which waited for: 5 -> 5; matrix products, arithmetic and copies ran while one was open for 13% -> 10% of each run, Pallas kernels for 16% -> 15%
where the time goes in v4:
time: 74.5 us; the launch traced here: 74.1 us
  waiting for transfers between devices  28.5 us (38%)
  starting transfers between devices  18.1 us (24%)
  Pallas kernels  15.7 us (21%)
  local copies, waits for them, and re-layouts  4.54 us (6%)
  other arithmetic  3.63 us (5%)
  between operations  2.23 us (3%)
  matrix products  1.32 us (2%)
    ppermute x11, waiting for transfers between devices, moved(): return lax.ppermute(chunk, 'replica', pairs)  27.3 us
    ppermute x11, starting transfers between devices, moved(): return lax.ppermute(chunk, 'replica', pairs)  16.5 us
    pallas_call x1, Pallas kernels, attend_first(): pl.pallas_call(functools.partial(first_kernel, shape, read_flags, cuts, r...  9.55 us
    pallas_call x1, Pallas kernels, attend_last(): pl.pallas_call(functools.partial(last_kernel, shape, read_flags, routes),...  4.93 us
    select_n x3, other arithmetic, line_attention(): jnp.where(wish_far > 0, held, mine)  2.97 us
    slice x4, local copies, waits for them, and re-layouts, line_attention(): page[unit * sum(PARTS[:k]):unit * sum(PARTS[:k + 1])]  2.39 us
    ppermute x2, starting transfers between devices, swap_sum(): lax.ppermute(value, axis, [(i, i ^ step) for i in range(size)])  1.56 us
  transfers between devices with their start and end apart: 13, of which 5 were waited for; matrix products, arithmetic and copies ran while one was open for 10% of the time, Pallas kernels for 15%

profile of v4, /device:TPU:0, one launch (start us, length us, event | category | flops | bytes accessed | tf_op | source)
XLA Modules:
  0.0 74.1 jit_solution(8271629978356248440)
XLA Ops:
  0.0 1.1 %slice.13 = bf16[1,128,2,256]{3,2,1,0:T(2,128)(2,1)S(1)} slice(bf16[1,1024,2,256]{3,2,1,0:T(2,128)(2,1)} %param.14), slice={[0:1], [0:128], [0:2], [0:256]} | slice | bytes 262144 | tf_op jit(solution)/shard_map/slice | solution.py:232
  1.2 3.1 %collective-permute-start = (bf16[128,512]{1,0:T(8,128)(2,1)S(1)}, bf16[128,512]{1,0:T(8,128)(2,1)S(1)}, u32[]{:S(2)}, u32[]{:S(2)}) collective-permute-start(bf16[128,512]{1,0:T(8,128)(2,1)S(1)} %bitcast.31), channel_id=1, source_target_pairs={{0,4},{4,0},{8,12},{12,8},{1,5},{5,1},{9,13},{13,9},{2,6},{6,2},{1... | collective-permute-start | bytes 393224 | tf_op jit(solution)/shard_map/ppermute | solution.py:217
  4.9 1.3 %wish.1 = f32[1,512]{1,0:T(1,128)} custom-call(s32[4]{0:T(128)} %places_ref.1, s32[1]{0:T(128)} %copy.16.tenant_ref, bf16[128,512]{1,0:T(8,128)(2,1)} %bitcast.32), custom_call_target="tpu_custom_call" | custom-call | tf_op jit(solution)/shard_map/wish/pallas_call | solution.py:202
  6.2 4.5 %collective-permute-start.2 = (f32[1,512]{1,0:T(1,128)}, f32[1,512]{1,0:T(1,128)S(1)}, u32[]{:S(2)}, u32[]{:S(2)}) collective-permute-start(f32[1,512]{1,0:T(1,128)} %wish.1), channel_id=1, source_target_pairs={{12,4},{0,8},{13,5},{1,9},{14,6},{2,10},{15,7},{3,11},{28,20},{16,... | collective-permute-start | bytes 6152 | tf_op jit(solution)/shard_map/ppermute | solution.py:217
  11.3 1.3 %slice.12 = bf16[1,384,2,256]{3,2,1,0:T(2,128)(2,1)S(1)} slice(bf16[1,1024,2,256]{3,2,1,0:T(2,128)(2,1)} %param.14), slice={[0:1], [128:512], [0:2], [0:256]} | slice | bytes 786432 | tf_op jit(solution)/shard_map/slice | solution.py:232
  12.7 1.6 %collective-permute-start.3 = (bf16[384,512]{1,0:T(8,128)(2,1)S(1)}, bf16[384,512]{1,0:T(8,128)(2,1)S(1)}, u32[]{:S(2)}, u32[]{:S(2)}) collective-permute-start(bf16[384,512]{1,0:T(8,128)(2,1)S(1)} %bitcast.28), channel_id=1, source_target_pairs={{0,4},{4,0},{8,12},{12,8},{1,5},{5,1},{9,13},{13,9},{2,6},{6,2},{1... | collective-permute-start | bytes 1179656 | tf_op jit(solution)/shard_map/ppermute | solution.py:217
  14.3 0.9 %broadcast_select_fusion.4 = (bf16[128,512]{1,0:T(8,128)(2,1)S(1)}, bf16[128,512]{1,0:T(8,128)(2,1)S(1)}) fusion(bf16[128,512]{1,0:T(8,128)(2,1)S(1)} %collective-permute-done.refs_8_, bf16[128,512]{1,0:T(8,128)(2,1)} %bitcast.33, pred[512]{0:T(512)(128)(4,1)S(1)} %compare_reduce_fusion, pred[512]{0:T(512)(128)(4,1)S(1)} %compare_reduce_fusion.1), kind=kLoop, calls=%fused_computation.7 | loop fusion | flops 131072 | bytes 525312 | tf_op jit(solution)/shard_map/jit(_where)/select_n | solution.py:250
  15.9 1.3 %collective-permute-start.5 = (bf16[128,512]{1,0:T(8,128)(2,1)S(1)}, bf16[128,512]{1,0:T(8,128)(2,1)S(1)}, u32[]{:S(2)}, u32[]{:S(2)}) collective-permute-start(bf16[128,512]{1,0:T(8,128)(2,1)S(1)} %get-tuple-element.33), channel_id=1, source_target_pairs={{4,12},{8,0},{5,13},{9,1},{6,14},{10,2},{7,15},{11,3},{20,28},{24,... | collective-permute-start | bytes 393224 | tf_op jit(solution)/shard_map/ppermute | solution.py:217
  17.3 7.1 %collective-permute-done.5.refs_10_ = bf16[128,512]{1,0:T(8,128)(2,1)S(1)} collective-permute-done((bf16[128,512]{1,0:T(8,128)(2,1)S(1)}, bf16[128,512]{1,0:T(8,128)(2,1)S(1)}, u32[]{:S(2)}, u32[]{:S(2)}) %collective-permute-start.5) | collective-permute-done | bytes 131104 | tf_op jit(solution)/shard_map/ppermute | solution.py:217
  24.4 1.5 %collective-permute-done.3.refs_12_ = bf16[384,512]{1,0:T(8,128)(2,1)S(1)} collective-permute-done((bf16[384,512]{1,0:T(8,128)(2,1)S(1)}, bf16[384,512]{1,0:T(8,128)(2,1)S(1)}, u32[]{:S(2)}, u32[]{:S(2)}) %collective-permute-start.3) | collective-permute-done | bytes 393248 | tf_op jit(solution)/shard_map/ppermute | solution.py:217
  25.9 1.0 %broadcast_select_fusion.2 = (bf16[384,512]{1,0:T(8,128)(2,1)}, bf16[384,512]{1,0:T(8,128)(2,1)}) fusion(bf16[384,512]{1,0:T(8,128)(2,1)S(1)} %collective-permute-done.3.refs_12_, bf16[384,512]{1,0:T(8,128)(2,1)S(1)} %bitcast.29, pred[512]{0:T(512)(128)(4,1)S(1)} %compare_reduce_fusion, pred[512]{0:T(512)(128)(4,1)S(1)} %compare_reduce_fusion.1), kind=kLoop, calls=%fused_computation.2 | loop fusion | flops 393216 | bytes 1573888 | tf_op jit(solution)/shard_map/jit(_where)/select_n | solution.py:250
  27.0 1.4 %collective-permute-start.6 = (bf16[384,512]{1,0:T(8,128)(2,1)}, bf16[384,512]{1,0:T(8,128)(2,1)}, u32[]{:S(2)}, u32[]{:S(2)}) collective-permute-start(bf16[384,512]{1,0:T(8,128)(2,1)} %get-tuple-element.32), channel_id=1, source_target_pairs={{4,8},{8,4},{5,9},{9,5},{6,10},{10,6},{7,11},{11,7},{20,24},{24,20... | collective-permute-start | bytes 1179656 | tf_op jit(solution)/shard_map/ppermute | solution.py:217
  28.4 1.3 %collective-permute-start.9 = (bf16[384,512]{1,0:T(8,128)(2,1)}, bf16[384,512]{1,0:T(8,128)(2,1)}, u32[]{:S(2)}, u32[]{:S(2)}) collective-permute-start(bf16[384,512]{1,0:T(8,128)(2,1)} %get-tuple-element.31), channel_id=1, source_target_pairs={{4,12},{8,0},{5,13},{9,1},{6,14},{10,2},{7,15},{11,3},{20,28},{24,... | collective-permute-start | bytes 1179656 | tf_op jit(solution)/shard_map/ppermute | solution.py:217
  29.7 11.9 %collective-permute-done.10.refs_7_ = bf16[512,512]{1,0:T(8,128)(2,1)S(1)} collective-permute-done((bf16[512,512]{1,0:T(8,128)(2,1)S(1)}, bf16[512,512]{1,0:T(8,128)(2,1)S(1)}, u32[]{:S(2)}, u32[]{:S(2)}) %collective-permute-start.10) | collective-permute-done | bytes 524320 | tf_op jit(solution)/shard_map/ppermute | solution.py:217
  41.7 1.0 %broadcast_select_fusion = (bf16[512,512]{1,0:T(8,128)(2,1)}, bf16[512,512]{1,0:T(8,128)(2,1)}) fusion(bf16[512,512]{1,0:T(8,128)(2,1)S(1)} %collective-permute-done.10.refs_7_, bf16[512,512]{1,0:T(8,128)(2,1)S(1)} %bitcast.24, pred[512]{0:T(512)(128)(4,1)S(1)} %compare_reduce_fusion, pred[512]{0:T(512)(128)(4,1)S(1)} %compare_reduce_fusion.1), kind=kLoop, calls=%fused_computation | loop fusion | flops 524288 | bytes 2098176 | tf_op jit(solution)/shard_map/jit(_where)/select_n | solution.py:250
  42.7 0.7 collective-permute-start.11
  43.4 1.3 %collective-permute-start.12 = (bf16[512,512]{1,0:T(8,128)(2,1)}, bf16[512,512]{1,0:T(8,128)(2,1)S(1)}, u32[]{:S(2)}, u32[]{:S(2)}) collective-permute-start(bf16[512,512]{1,0:T(8,128)(2,1)} %get-tuple-element.29), channel_id=1, source_target_pairs={{4,12},{8,0},{5,13},{9,1},{6,14},{10,2},{7,15},{11,3},{20,28},{24,... | collective-permute-start | bytes 1572872 | tf_op jit(solution)/shard_map/ppermute | solution.py:217
  45.4 1.3 %fusion = f32[32,256]{1,0:T(8,128)S(1)} fusion(bf16[256,2048]{1,0:T(8,128)(2,1)S(1)} %copy-done, bf16[2,32,2048]{2,1,0:T(8,128)(2,1)} %param.15, s32[]{:T(128)S(6)} %select_n.29), kind=kOutput, calls=%fused_computation.4 | convolution fusion | flops 33554432 | bytes 1212420 | tf_op jit(solution)/shard_map/dot_general | solution.py:309
  46.8 1.2 %collective-permute-done.7 = f32[32,256]{1,0:T(8,128)S(1)} collective-permute-done((f32[32,256]{1,0:T(8,128)S(1)}, f32[32,256]{1,0:T(8,128)S(1)}, u32[]{:S(2)}, u32[]{:S(2)}) %collective-permute-start.7) | collective-permute-done | bytes 32800 | tf_op jit(solution)/shard_map/ppermute | solution.py:24
  48.0 1.5 %collective-permute-start.8 = (f32[32,256]{1,0:T(8,128)S(1)}, f32[32,256]{1,0:T(8,128)S(1)}, u32[]{:S(2)}, u32[]{:S(2)}) collective-permute-start(f32[32,256]{1,0:T(8,128)S(1)} %add.15), channel_id=1, source_target_pairs={{0,2},{1,3},{2,0},{3,1},{4,6},{5,7},{6,4},{7,5},{8,10},{9,11},{10,... | collective-permute-start | bytes 98312 | tf_op jit(solution)/shard_map/ppermute | solution.py:24
  51.4 0.7 %copy.14 = bf16[32,8,2,256]{3,1,2,0:T(8,128)(2,1)} copy(bf16[32,8,2,256]{3,2,1,0:T(2,128)(2,1)S(1)} %bitcast.36) | data formatting | bytes 524288
  52.7 9.6 %attend_first.1 = (bf16[256,2048]{1,0:T(8,128)(2,1)S(1)}, f32[256,2048]{1,0:T(8,128)S(1)}, f32[256,2048]{1,0:T(8,128)S(1)}, f32[256,2048]{1,0:T(8,128)S(1)}) custom-call(s32[1]{0:T(128)} %dynamic_slice.7.refs_0_, s32[1]{0:T(128)} %copy.18.refs_1_, f32[32,256]{1,0:T(8,128)} %add.16.refs_2_, bf16[256,2048]{1,0:T(8,128)(2,1)} %refs_3_.1, ...), custom_call_target="tpu_custom_call" | custom-call | flops 1610612736 | bytes 2097152 | tf_op jit(solution)/shard_map/attend_first/pallas_call | solution.py:171
  62.3 6.8 %collective-permute-done.12.refs_9_ = bf16[512,512]{1,0:T(8,128)(2,1)S(1)} collective-permute-done((bf16[512,512]{1,0:T(8,128)(2,1)}, bf16[512,512]{1,0:T(8,128)(2,1)S(1)}, u32[]{:S(2)}, u32[]{:S(2)}) %collective-permute-start.12) | collective-permute-done | bytes 524320 | tf_op jit(solution)/shard_map/ppermute | solution.py:217
  69.1 4.9 %attend_last.1 = bf16[256,2048]{1,0:T(8,128)(2,1)} custom-call(s32[1]{0:T(128)} %dynamic_slice.7.refs_0_, s32[1]{0:T(128)S(6)} %copy.17.refs_1_, bf16[256,2048]{1,0:T(8,128)(2,1)S(1)} %get-tuple-element.22.refs_2_, f32[256,2048]{1,0:T(8,128)S(1)} %get-tuple-element.23.refs_3_, f32[256,2048]{1,0:T(8,128)S(1)} %get-tuple-element.24.refs_4_, ...), custom_call_target="tpu_custom_call" | custom-call | flops 1073741824 | bytes 2097152 | tf_op jit(solution)/shard_map/attend_last/pallas_call | solution.py:189
  (43 shorter events, 3.6 us)
Async XLA Ops:
  0.0 45.4 %copy-start = (bf16[256,2048]{1,0:T(8,128)(2,1)S(1)}, bf16[256,2048]{1,0:T(8,128)(2,1)}, u32[]{:S(2)}) copy-start(bf16[256,2048]{1,0:T(8,128)(2,1)} %param.11) | copy-start | bytes 3145732
  0.0 17.2 %slice-start = ((bf16[1,1024,2,256]{3,2,1,0:T(2,128)(2,1)}), bf16[1,512,2,256]{3,2,1,0:T(2,128)(2,1)S(1)}, s32[]{:S(2)}) async-start(bf16[1,1024,2,256]{3,2,1,0:T(2,128)(2,1)} %param.14), calls=%async_computation | async-start | bytes 1048576 | tf_op jit(solution)/shard_map/slice | solution.py:232
  1.1 3.8 %copy-start.2 = (bf16[16,8,2,256]{3,1,2,0:T(8,128)(2,1)}, bf16[16,8,2,256]{3,1,2,0:T(8,128)(2,1)S(1)}, u32[]{:S(2)}) copy-start(bf16[16,8,2,256]{3,1,2,0:T(8,128)(2,1)S(1)} %copy.13) | copy-start | bytes 393220
  1.2 11.6 %collective-permute-start = (bf16[128,512]{1,0:T(8,128)(2,1)S(1)}, bf16[128,512]{1,0:T(8,128)(2,1)S(1)}, u32[]{:S(2)}, u32[]{:S(2)}) collective-permute-start(bf16[128,512]{1,0:T(8,128)(2,1)S(1)} %bitcast.31), channel_id=1, source_target_pairs={{0,4},{4,0},{8,12},{12,8},{1,5},{5,1},{9,13},{13,9},{2,6},{6,2},{1... | collective-permute-start | bytes 393224 | tf_op jit(solution)/shard_map/ppermute | solution.py:217
  6.2 6.5 %collective-permute-start.2 = (f32[1,512]{1,0:T(1,128)}, f32[1,512]{1,0:T(1,128)S(1)}, u32[]{:S(2)}, u32[]{:S(2)}) collective-permute-start(f32[1,512]{1,0:T(1,128)} %wish.1), channel_id=1, source_target_pairs={{12,4},{0,8},{13,5},{1,9},{14,6},{2,10},{15,7},{3,11},{28,20},{16,... | collective-permute-start | bytes 6152 | tf_op jit(solution)/shard_map/ppermute | solution.py:217
  10.7 2.0 %collective-permute-start.1 = (f32[1,512]{1,0:T(1,128)}, f32[1,512]{1,0:T(1,128)S(1)}, u32[]{:S(2)}, u32[]{:S(2)}) collective-permute-start(f32[1,512]{1,0:T(1,128)} %wish.1), channel_id=1, source_target_pairs={{4,8},{8,4},{5,9},{9,5},{6,10},{10,6},{7,11},{11,7},{20,24},{24,20... | collective-permute-start | bytes 6152 | tf_op jit(solution)/shard_map/ppermute | solution.py:217
  12.7 14.2 %copy-start.1 = (bf16[48,8,2,256]{3,1,2,0:T(8,128)(2,1)}, bf16[48,8,2,256]{3,1,2,0:T(8,128)(2,1)S(1)}, u32[]{:S(2)}) copy-start(bf16[48,8,2,256]{3,1,2,0:T(8,128)(2,1)S(1)} %copy.12) | copy-start | bytes 1179652
  12.7 14.2 %copy-start.5 = (bf16[128,512]{1,0:T(8,128)(2,1)}, bf16[128,512]{1,0:T(8,128)(2,1)S(1)}, u32[]{:S(2)}) copy-start(bf16[128,512]{1,0:T(8,128)(2,1)S(1)} %collective-permute-done.refs_8_) | copy-start | bytes 393220
  12.7 13.2 %collective-permute-start.3 = (bf16[384,512]{1,0:T(8,128)(2,1)S(1)}, bf16[384,512]{1,0:T(8,128)(2,1)S(1)}, u32[]{:S(2)}, u32[]{:S(2)}) collective-permute-start(bf16[384,512]{1,0:T(8,128)(2,1)S(1)} %bitcast.28), channel_id=1, source_target_pairs={{0,4},{4,0},{8,12},{12,8},{1,5},{5,1},{9,13},{13,9},{2,6},{6,2},{1... | collective-permute-start | bytes 1179656 | tf_op jit(solution)/shard_map/ppermute | solution.py:217
  15.2 2.1 %collective-permute-start.4 = (bf16[128,512]{1,0:T(8,128)(2,1)S(1)}, bf16[128,512]{1,0:T(8,128)(2,1)S(1)}, u32[]{:S(2)}, u32[]{:S(2)}) collective-permute-start(bf16[128,512]{1,0:T(8,128)(2,1)S(1)} %get-tuple-element.34), channel_id=1, source_target_pairs={{4,8},{8,4},{5,9},{9,5},{6,10},{10,6},{7,11},{11,7},{20,24},{24,20... | collective-permute-start | bytes 393224 | tf_op jit(solution)/shard_map/ppermute | solution.py:217
  15.9 8.5 %collective-permute-start.5 = (bf16[128,512]{1,0:T(8,128)(2,1)S(1)}, bf16[128,512]{1,0:T(8,128)(2,1)S(1)}, u32[]{:S(2)}, u32[]{:S(2)}) collective-permute-start(bf16[128,512]{1,0:T(8,128)(2,1)S(1)} %get-tuple-element.33), channel_id=1, source_target_pairs={{4,12},{8,0},{5,13},{9,1},{6,14},{10,2},{7,15},{11,3},{20,28},{24,... | collective-permute-start | bytes 393224 | tf_op jit(solution)/shard_map/ppermute | solution.py:217
  17.3 26.1 %copy-start.8 = (bf16[128,512]{1,0:T(8,128)(2,1)}, bf16[128,512]{1,0:T(8,128)(2,1)S(1)}, u32[]{:S(2)}) copy-start(bf16[128,512]{1,0:T(8,128)(2,1)S(1)} %collective-permute-done.4.refs_9_) | copy-start | bytes 393220
  24.4 19.0 %copy-start.9 = (bf16[128,512]{1,0:T(8,128)(2,1)}, bf16[128,512]{1,0:T(8,128)(2,1)S(1)}, u32[]{:S(2)}) copy-start(bf16[128,512]{1,0:T(8,128)(2,1)S(1)} %collective-permute-done.5.refs_10_) | copy-start | bytes 393220
  25.9 16.8 %copy-start.3 = (bf16[384,512]{1,0:T(8,128)(2,1)}, bf16[384,512]{1,0:T(8,128)(2,1)S(1)}, u32[]{:S(2)}) copy-start(bf16[384,512]{1,0:T(8,128)(2,1)S(1)} %collective-permute-done.3.refs_12_) | copy-start | bytes 1179652
  26.9 23.8 %copy-start.6 = (bf16[2,16,2,128]{3,2,1,0:T(2,128)(2,1)S(1)}, bf16[2,16,2,128]{3,2,1,0:T(2,128)(2,1)}, u32[]{:S(2)}) copy-start(bf16[2,16,2,128]{3,2,1,0:T(2,128)(2,1)} %param.17) | copy-start | bytes 49156
  26.9 22.6 %copy-start.7 = (s32[4]{0:T(128)S(1)}, s32[4]{0:T(128)}, u32[]{:S(2)}) copy-start(s32[4]{0:T(128)} %places_ref.1) | copy-start | bytes 52
  26.9 24.5 %copy-start.4 = (bf16[256,2,256]{2,1,0:T(2,128)(2,1)S(1)}, bf16[256,2,256]{2,1,0:T(2,128)(2,1)}, u32[]{:S(2)}) copy-start(bf16[256,2,256]{2,1,0:T(2,128)(2,1)} %param.13) | copy-start | bytes 786436
  26.9 14.7 %collective-permute-start.10 = (bf16[512,512]{1,0:T(8,128)(2,1)S(1)}, bf16[512,512]{1,0:T(8,128)(2,1)S(1)}, u32[]{:S(2)}, u32[]{:S(2)}) collective-permute-start(bf16[512,512]{1,0:T(8,128)(2,1)S(1)} %bitcast.23), channel_id=1, source_target_pairs={{0,4},{4,0},{8,12},{12,8},{1,5},{5,1},{9,13},{13,9},{2,6},{6,2},{1... | collective-permute-start | bytes 1572872 | tf_op jit(solution)/shard_map/ppermute | solution.py:217
  27.0 18.4 %collective-permute-start.6 = (bf16[384,512]{1,0:T(8,128)(2,1)}, bf16[384,512]{1,0:T(8,128)(2,1)}, u32[]{:S(2)}, u32[]{:S(2)}) collective-permute-start(bf16[384,512]{1,0:T(8,128)(2,1)} %get-tuple-element.32), channel_id=1, source_target_pairs={{4,8},{8,4},{5,9},{9,5},{6,10},{10,6},{7,11},{11,7},{20,24},{24,20... | collective-permute-start | bytes 1179656 | tf_op jit(solution)/shard_map/ppermute | solution.py:217
  28.4 24.3 %collective-permute-start.9 = (bf16[384,512]{1,0:T(8,128)(2,1)}, bf16[384,512]{1,0:T(8,128)(2,1)}, u32[]{:S(2)}, u32[]{:S(2)}) collective-permute-start(bf16[384,512]{1,0:T(8,128)(2,1)} %get-tuple-element.31), channel_id=1, source_target_pairs={{4,12},{8,0},{5,13},{9,1},{6,14},{10,2},{7,15},{11,3},{20,28},{24,... | collective-permute-start | bytes 1179656 | tf_op jit(solution)/shard_map/ppermute | solution.py:217
  42.7 19.6 %collective-permute-start.11 = (bf16[512,512]{1,0:T(8,128)(2,1)}, bf16[512,512]{1,0:T(8,128)(2,1)S(1)}, u32[]{:S(2)}, u32[]{:S(2)}) collective-permute-start(bf16[512,512]{1,0:T(8,128)(2,1)} %get-tuple-element.30), channel_id=1, source_target_pairs={{4,8},{8,4},{5,9},{9,5},{6,10},{10,6},{7,11},{11,7},{20,24},{24,20... | collective-permute-start | bytes 1572872 | tf_op jit(solution)/shard_map/ppermute | solution.py:217
  43.4 25.7 %collective-permute-start.12 = (bf16[512,512]{1,0:T(8,128)(2,1)}, bf16[512,512]{1,0:T(8,128)(2,1)S(1)}, u32[]{:S(2)}, u32[]{:S(2)}) collective-permute-start(bf16[512,512]{1,0:T(8,128)(2,1)} %get-tuple-element.29), channel_id=1, source_target_pairs={{4,12},{8,0},{5,13},{9,1},{6,14},{10,2},{7,15},{11,3},{20,28},{24,... | collective-permute-start | bytes 1572872 | tf_op jit(solution)/shard_map/ppermute | solution.py:217
  46.7 1.3 %collective-permute-start.7 = (f32[32,256]{1,0:T(8,128)S(1)}, f32[32,256]{1,0:T(8,128)S(1)}, u32[]{:S(2)}, u32[]{:S(2)}) collective-permute-start(f32[32,256]{1,0:T(8,128)S(1)} %fusion), channel_id=1, source_target_pairs={{0,1},{1,0},{2,3},{3,2},{4,5},{5,4},{6,7},{7,6},{8,9},{9,8},{10,11... | collective-permute-start | bytes 98312 | tf_op jit(solution)/shard_map/ppermute | solution.py:24
  48.0 4.1 %collective-permute-start.8 = (f32[32,256]{1,0:T(8,128)S(1)}, f32[32,256]{1,0:T(8,128)S(1)}, u32[]{:S(2)}, u32[]{:S(2)}) collective-permute-start(f32[32,256]{1,0:T(8,128)S(1)} %add.15), channel_id=1, source_target_pairs={{0,2},{1,3},{2,0},{3,1},{4,6},{5,7},{6,4},{7,5},{8,10},{9,11},{10,... | collective-permute-start | bytes 98312 | tf_op jit(solution)/shard_map/ppermute | solution.py:24

commit v5 on v4

--- a/solution.py
+++ b/solution.py
@@ -210,7 +210,7 @@
 
 EDGES, MIDDLE, FAR = [(0, 1), (1, 0), (2, 3), (3, 2)], [(1, 2), (2, 1)], [(1, 3), (2, 0)]
 TO_INSIDE = [(3, 1), (0, 2)]
-PARTS = (1, 3, 4)
+PARTS = (3, 7, 6)
 
 
 def moved(chunk, pairs):

time: 74.5 us -> 73.8 us (level)
  Pallas kernels: 15.7 us -> 17.9 us
  waiting for transfers between devices: 28.5 us -> 26.3 us
  starting transfers between devices: 18.1 us -> 17.1 us
    ppermute x11, waiting for transfers between devices: 27.3 us -> 25.1 us  [moved(): return lax.ppermute(chunk, 'replica', pairs)]
    ppermute x2, starting transfers between devices: 1.56 us -> 0.07 us  [swap_sum(): lax.ppermute(value, axis, [(i, i ^ step) for i in range(size)])]
    pallas_call x1, Pallas kernels: 9.55 us -> 10.8 us  [attend_first(): pl.pallas_call(functools.partial(first_kernel, shape, read_flags, cuts, r...]
    slice x4 -> x5, local copies, waits for them, and re-layouts: 2.39 us -> 1.19 us  [line_attention(): page[unit * sum(PARTS[:k]):unit * sum(PARTS[:k + 1])]]
    unnamed x24 -> x20, local copies, waits for them, and re-layouts: 0.95 us -> 1.86 us
    pallas_call x1, Pallas kernels: 4.93 us -> 5.84 us  [attend_last(): pl.pallas_call(functools.partial(last_kernel, shape, read_flags, routes),...]
  transfers between devices with their start and end apart: 13 -> 13, of which waited for: 5 -> 7; matrix products, arithmetic and copies ran while one was open for 10% -> 10% of each run, Pallas kernels for 15% -> 16%
where the time goes in v5:
time: 73.8 us; the launch traced here: 73.3 us
  waiting for transfers between devices  26.3 us (36%)
  Pallas kernels  17.9 us (24%)
  starting transfers between devices  17.1 us (23%)
  local copies, waits for them, and re-layouts  4.93 us (7%)
  other arithmetic  3.47 us (5%)
  between operations  2.25 us (3%)
  matrix products  1.32 us (2%)
    ppermute x11, waiting for transfers between devices, moved(): return lax.ppermute(chunk, 'replica', pairs)  25.1 us
    ppermute x11, starting transfers between devices, moved(): return lax.ppermute(chunk, 'replica', pairs)  17.1 us
    pallas_call x1, Pallas kernels, attend_first(): pl.pallas_call(functools.partial(first_kernel, shape, read_flags, cuts, r...  10.8 us
    pallas_call x1, Pallas kernels, attend_last(): pl.pallas_call(functools.partial(last_kernel, shape, read_flags, routes),...  5.84 us
    select_n x3, other arithmetic, line_attention(): jnp.where(wish_far > 0, held, mine)  2.81 us
    unnamed x20, local copies, waits for them, and re-layouts  1.86 us
  transfers between devices with their start and end apart: 13, of which 7 were waited for; matrix products, arithmetic and copies ran while one was open for 10% of the time, Pallas kernels for 16%

profile of v5, /device:TPU:0, one launch (start us, length us, event | category | flops | bytes accessed | tf_op | source)
XLA Modules:
  0.0 73.3 jit_solution(1728526804786714775)
XLA Ops:
  0.0 1.2 %slice.13 = bf16[1,192,2,256]{3,2,1,0:T(2,128)(2,1)S(1)} slice(bf16[1,1024,2,256]{3,2,1,0:T(2,128)(2,1)} %param.14), slice={[0:1], [0:192], [0:2], [0:256]} | slice | bytes 393216 | tf_op jit(solution)/shard_map/slice | solution.py:232
  1.2 3.1 %collective-permute-start = (bf16[192,512]{1,0:T(8,128)(2,1)S(1)}, bf16[192,512]{1,0:T(8,128)(2,1)S(1)}, u32[]{:S(2)}, u32[]{:S(2)}) collective-permute-start(bf16[192,512]{1,0:T(8,128)(2,1)S(1)} %bitcast.31), channel_id=1, source_target_pairs={{0,4},{4,0},{8,12},{12,8},{1,5},{5,1},{9,13},{13,9},{2,6},{6,2},{1... | collective-permute-start | bytes 589832 | tf_op jit(solution)/shard_map/ppermute | solution.py:217
  5.0 1.3 %wish.1 = f32[1,512]{1,0:T(1,128)} custom-call(s32[4]{0:T(128)} %places_ref.1, s32[1]{0:T(128)} %copy.16.tenant_ref, bf16[192,512]{1,0:T(8,128)(2,1)} %bitcast.32), custom_call_target="tpu_custom_call" | custom-call | tf_op jit(solution)/shard_map/wish/pallas_call | solution.py:202
  6.2 4.5 %collective-permute-start.2 = (f32[1,512]{1,0:T(1,128)}, f32[1,512]{1,0:T(1,128)S(1)}, u32[]{:S(2)}, u32[]{:S(2)}) collective-permute-start(f32[1,512]{1,0:T(1,128)} %wish.1), channel_id=1, source_target_pairs={{12,4},{0,8},{13,5},{1,9},{14,6},{2,10},{15,7},{3,11},{28,20},{16,... | collective-permute-start | bytes 6152 | tf_op jit(solution)/shard_map/ppermute | solution.py:217
  11.5 0.7 %collective-permute-done.2 = f32[1,512]{1,0:T(1,128)S(1)} collective-permute-done((f32[1,512]{1,0:T(1,128)}, f32[1,512]{1,0:T(1,128)S(1)}, u32[]{:S(2)}, u32[]{:S(2)}) %collective-permute-start.2) | collective-permute-done | bytes 2080 | tf_op jit(solution)/shard_map/ppermute | solution.py:217
  12.3 2.1 %collective-permute-start.3 = (bf16[448,512]{1,0:T(8,128)(2,1)S(1)}, bf16[448,512]{1,0:T(8,128)(2,1)S(1)}, u32[]{:S(2)}, u32[]{:S(2)}) collective-permute-start(bf16[448,512]{1,0:T(8,128)(2,1)S(1)} %bitcast.28), channel_id=1, source_target_pairs={{0,4},{4,0},{8,12},{12,8},{1,5},{5,1},{9,13},{13,9},{2,6},{6,2},{1... | collective-permute-start | bytes 1376264 | tf_op jit(solution)/shard_map/ppermute | solution.py:217
  14.4 1.0 %broadcast_select_fusion.4 = (bf16[192,512]{1,0:T(8,128)(2,1)S(1)}, bf16[192,512]{1,0:T(8,128)(2,1)S(1)}) fusion(bf16[192,512]{1,0:T(8,128)(2,1)S(1)} %collective-permute-done.refs_8_, bf16[192,512]{1,0:T(8,128)(2,1)} %bitcast.33, pred[512]{0:T(512)(128)(4,1)S(1)} %compare_reduce_fusion, pred[512]{0:T(512)(128)(4,1)S(1)} %compare_reduce_fusion.1), kind=kLoop, calls=%fused_computation.4 | loop fusion | flops 196608 | bytes 787456 | tf_op jit(solution)/shard_map/jit(_where)/select_n | solution.py:250
  16.0 1.3 %collective-permute-start.5 = (bf16[192,512]{1,0:T(8,128)(2,1)S(1)}, bf16[192,512]{1,0:T(8,128)(2,1)S(1)}, u32[]{:S(2)}, u32[]{:S(2)}) collective-permute-start(bf16[192,512]{1,0:T(8,128)(2,1)S(1)} %get-tuple-element.33), channel_id=1, source_target_pairs={{4,12},{8,0},{5,13},{9,1},{6,14},{10,2},{7,15},{11,3},{20,28},{24,... | collective-permute-start | bytes 589832 | tf_op jit(solution)/shard_map/ppermute | solution.py:217
  17.4 9.1 %collective-permute-done.5.refs_10_ = bf16[192,512]{1,0:T(8,128)(2,1)S(1)} collective-permute-done((bf16[192,512]{1,0:T(8,128)(2,1)S(1)}, bf16[192,512]{1,0:T(8,128)(2,1)S(1)}, u32[]{:S(2)}, u32[]{:S(2)}) %collective-permute-start.5) | collective-permute-done | bytes 196640 | tf_op jit(solution)/shard_map/ppermute | solution.py:217
  26.5 1.7 %collective-permute-done.3.refs_12_ = bf16[448,512]{1,0:T(8,128)(2,1)S(1)} collective-permute-done((bf16[448,512]{1,0:T(8,128)(2,1)S(1)}, bf16[448,512]{1,0:T(8,128)(2,1)S(1)}, u32[]{:S(2)}, u32[]{:S(2)}) %collective-permute-start.3) | collective-permute-done | bytes 458784 | tf_op jit(solution)/shard_map/ppermute | solution.py:217
  28.2 1.0 %broadcast_select_fusion = (bf16[448,512]{1,0:T(8,128)(2,1)}, bf16[448,512]{1,0:T(8,128)(2,1)}) fusion(bf16[448,512]{1,0:T(8,128)(2,1)S(1)} %collective-permute-done.3.refs_12_, bf16[448,512]{1,0:T(8,128)(2,1)S(1)} %bitcast.29, pred[512]{0:T(512)(128)(4,1)S(1)} %compare_reduce_fusion, pred[512]{0:T(512)(128)(4,1)S(1)} %compare_reduce_fusion.1), kind=kLoop, calls=%fused_computation | loop fusion | flops 458752 | bytes 1836032 | tf_op jit(solution)/shard_map/jit(_where)/select_n | solution.py:250
  29.3 1.4 %collective-permute-start.6 = (bf16[448,512]{1,0:T(8,128)(2,1)}, bf16[448,512]{1,0:T(8,128)(2,1)}, u32[]{:S(2)}, u32[]{:S(2)}) collective-permute-start(bf16[448,512]{1,0:T(8,128)(2,1)} %get-tuple-element.30), channel_id=1, source_target_pairs={{4,8},{8,4},{5,9},{9,5},{6,10},{10,6},{7,11},{11,7},{20,24},{24,20... | collective-permute-start | bytes 1376264 | tf_op jit(solution)/shard_map/ppermute | solution.py:217
  31.4 1.3 %collective-permute-start.9 = (bf16[448,512]{1,0:T(8,128)(2,1)}, bf16[448,512]{1,0:T(8,128)(2,1)}, u32[]{:S(2)}, u32[]{:S(2)}) collective-permute-start(bf16[448,512]{1,0:T(8,128)(2,1)} %get-tuple-element.29), channel_id=1, source_target_pairs={{4,12},{8,0},{5,13},{9,1},{6,14},{10,2},{7,15},{11,3},{20,28},{24,... | collective-permute-start | bytes 1376264 | tf_op jit(solution)/shard_map/ppermute | solution.py:217
  32.7 6.2 %collective-permute-done.10.refs_7_ = bf16[384,512]{1,0:T(8,128)(2,1)S(1)} collective-permute-done((bf16[384,512]{1,0:T(8,128)(2,1)S(1)}, bf16[384,512]{1,0:T(8,128)(2,1)S(1)}, u32[]{:S(2)}, u32[]{:S(2)}) %collective-permute-start.10) | collective-permute-done | bytes 393248 | tf_op jit(solution)/shard_map/ppermute | solution.py:217
  39.0 0.8 %broadcast_select_fusion.2 = (bf16[384,512]{1,0:T(8,128)(2,1)S(1)}, bf16[384,512]{1,0:T(8,128)(2,1)}) fusion(bf16[384,512]{1,0:T(8,128)(2,1)S(1)} %collective-permute-done.10.refs_7_, bf16[384,512]{1,0:T(8,128)(2,1)S(1)} %bitcast.24, pred[512]{0:T(512)(128)(4,1)S(1)} %compare_reduce_fusion, pred[512]{0:T(512)(128)(4,1)S(1)} %compare_reduce_fusion.1), kind=kLoop, calls=%fused_computation.2 | loop fusion | flops 393216 | bytes 1573888 | tf_op jit(solution)/shard_map/jit(_where)/select_n | solution.py:250
  39.8 0.7 collective-permute-start.11
  40.5 1.3 %collective-permute-start.12 = (bf16[384,512]{1,0:T(8,128)(2,1)S(1)}, bf16[384,512]{1,0:T(8,128)(2,1)S(1)}, u32[]{:S(2)}, u32[]{:S(2)}) collective-permute-start(bf16[384,512]{1,0:T(8,128)(2,1)S(1)} %get-tuple-element.31), channel_id=1, source_target_pairs={{4,12},{8,0},{5,13},{9,1},{6,14},{10,2},{7,15},{11,3},{20,28},{24,... | collective-permute-start | bytes 1179656 | tf_op jit(solution)/shard_map/ppermute | solution.py:217
  41.8 1.3 %fusion = f32[32,256]{1,0:T(8,128)S(1)} fusion(bf16[256,2048]{1,0:T(8,128)(2,1)S(1)} %copy-done, bf16[2,32,2048]{2,1,0:T(8,128)(2,1)} %param.15, s32[]{:T(128)S(6)} %select_n.29), kind=kOutput, calls=%fused_computation.6 | convolution fusion | flops 33554432 | bytes 1212420 | tf_op jit(solution)/shard_map/dot_general | solution.py:309
  43.2 1.2 %collective-permute-done.7 = f32[32,256]{1,0:T(8,128)S(1)} collective-permute-done((f32[32,256]{1,0:T(8,128)S(1)}, f32[32,256]{1,0:T(8,128)S(1)}, u32[]{:S(2)}, u32[]{:S(2)}) %collective-permute-start.7) | collective-permute-done | bytes 32800 | tf_op jit(solution)/shard_map/ppermute | solution.py:24
  44.4 1.3 %dynamic_slice.7.refs_0_ = s32[1]{0:T(128)} dynamic-slice(s32[4]{0:T(128)} %places_ref.1, s32[]{:T(128)S(6)} %select_n.28), dynamic_slice_sizes={1} | dynamic-slice | bytes 12 | tf_op jit(solution)/shard_map/dynamic_slice | solution.py:258
  47.0 1.7 %copy.14 = bf16[32,8,2,256]{3,1,2,0:T(8,128)(2,1)} copy(bf16[32,8,2,256]{3,2,1,0:T(2,128)(2,1)} %bitcast.36) | data formatting | bytes 524288
  49.2 7.0 %collective-permute-done.9.refs_14_ = bf16[448,512]{1,0:T(8,128)(2,1)} collective-permute-done((bf16[448,512]{1,0:T(8,128)(2,1)}, bf16[448,512]{1,0:T(8,128)(2,1)}, u32[]{:S(2)}, u32[]{:S(2)}) %collective-permute-start.9) | collective-permute-done | bytes 458784 | tf_op jit(solution)/shard_map/ppermute | solution.py:217
  56.3 10.8 %attend_first.1 = (bf16[256,2048]{1,0:T(8,128)(2,1)S(1)}, f32[256,2048]{1,0:T(8,128)S(1)}, f32[256,2048]{1,0:T(8,128)S(1)}, f32[256,2048]{1,0:T(8,128)S(1)}) custom-call(s32[1]{0:T(128)} %dynamic_slice.7.refs_0_, s32[1]{0:T(128)} %copy.18.refs_1_, f32[32,256]{1,0:T(8,128)} %add.16.refs_2_, bf16[256,2048]{1,0:T(8,128)(2,1)} %refs_3_.1, ...), custom_call_target="tpu_custom_call" | custom-call | flops 1879048192 | bytes 2097152 | tf_op jit(solution)/shard_map/attend_first/pallas_call | solution.py:171
  67.4 5.8 %attend_last.1 = bf16[256,2048]{1,0:T(8,128)(2,1)} custom-call(s32[1]{0:T(128)} %dynamic_slice.7.refs_0_, s32[1]{0:T(128)S(6)} %copy.17.refs_1_, bf16[256,2048]{1,0:T(8,128)(2,1)S(1)} %get-tuple-element.22.refs_2_, f32[256,2048]{1,0:T(8,128)S(1)} %get-tuple-element.23.refs_3_, f32[256,2048]{1,0:T(8,128)S(1)} %get-tuple-element.24.refs_4_, ...), custom_call_target="tpu_custom_call" | custom-call | flops 805306368 | bytes 2097152 | tf_op jit(solution)/shard_map/attend_last/pallas_call | solution.py:189
  (40 shorter events, 3.4 us)
Async XLA Ops:
  0.0 41.8 %copy-start = (bf16[256,2048]{1,0:T(8,128)(2,1)S(1)}, bf16[256,2048]{1,0:T(8,128)(2,1)}, u32[]{:S(2)}) copy-start(bf16[256,2048]{1,0:T(8,128)(2,1)} %param.11) | copy-start | bytes 3145732
  0.0 11.4 %slice-start = ((bf16[1,1024,2,256]{3,2,1,0:T(2,128)(2,1)}), bf16[1,448,2,256]{3,2,1,0:T(2,128)(2,1)S(1)}, s32[]{:S(2)}) async-start(bf16[1,1024,2,256]{3,2,1,0:T(2,128)(2,1)} %param.14), calls=%async_computation | async-start | bytes 917504 | tf_op jit(solution)/shard_map/slice | solution.py:232
  1.2 16.2 %slice-start.1 = ((bf16[1,1024,2,256]{3,2,1,0:T(2,128)(2,1)}), bf16[1,384,2,256]{3,2,1,0:T(2,128)(2,1)S(1)}, s32[]{:S(2)}) async-start(bf16[1,1024,2,256]{3,2,1,0:T(2,128)(2,1)} %param.14), calls=%async_computation.1 | async-start | bytes 786432 | tf_op jit(solution)/shard_map/slice | solution.py:232
  1.2 3.8 %copy-start.2 = (bf16[24,8,2,256]{3,1,2,0:T(8,128)(2,1)}, bf16[24,8,2,256]{3,1,2,0:T(8,128)(2,1)S(1)}, u32[]{:S(2)}) copy-start(bf16[24,8,2,256]{3,1,2,0:T(8,128)(2,1)S(1)} %copy.13) | copy-start | bytes 589828
  1.2 11.0 %collective-permute-start = (bf16[192,512]{1,0:T(8,128)(2,1)S(1)}, bf16[192,512]{1,0:T(8,128)(2,1)S(1)}, u32[]{:S(2)}, u32[]{:S(2)}) collective-permute-start(bf16[192,512]{1,0:T(8,128)(2,1)S(1)} %bitcast.31), channel_id=1, source_target_pairs={{0,4},{4,0},{8,12},{12,8},{1,5},{5,1},{9,13},{13,9},{2,6},{6,2},{1... | collective-permute-start | bytes 589832 | tf_op jit(solution)/shard_map/ppermute | solution.py:217
  6.2 6.0 %collective-permute-start.2 = (f32[1,512]{1,0:T(1,128)}, f32[1,512]{1,0:T(1,128)S(1)}, u32[]{:S(2)}, u32[]{:S(2)}) collective-permute-start(f32[1,512]{1,0:T(1,128)} %wish.1), channel_id=1, source_target_pairs={{12,4},{0,8},{13,5},{1,9},{14,6},{2,10},{15,7},{3,11},{28,20},{16,... | collective-permute-start | bytes 6152 | tf_op jit(solution)/shard_map/ppermute | solution.py:217
  10.7 1.5 %collective-permute-start.1 = (f32[1,512]{1,0:T(1,128)}, f32[1,512]{1,0:T(1,128)S(1)}, u32[]{:S(2)}, u32[]{:S(2)}) collective-permute-start(f32[1,512]{1,0:T(1,128)} %wish.1), channel_id=1, source_target_pairs={{4,8},{8,4},{5,9},{9,5},{6,10},{10,6},{7,11},{11,7},{20,24},{24,20... | collective-permute-start | bytes 6152 | tf_op jit(solution)/shard_map/ppermute | solution.py:217
  11.5 17.7 %copy-start.1 = (bf16[56,8,2,256]{3,1,2,0:T(8,128)(2,1)}, bf16[56,8,2,256]{3,1,2,0:T(8,128)(2,1)S(1)}, u32[]{:S(2)}) copy-start(bf16[56,8,2,256]{3,1,2,0:T(8,128)(2,1)S(1)} %copy.12) | copy-start | bytes 1376260
  12.3 16.9 %copy-start.4 = (bf16[192,512]{1,0:T(8,128)(2,1)}, bf16[192,512]{1,0:T(8,128)(2,1)S(1)}, u32[]{:S(2)}) copy-start(bf16[192,512]{1,0:T(8,128)(2,1)S(1)} %collective-permute-done.refs_8_) | copy-start | bytes 589828
  12.3 15.9 %collective-permute-start.3 = (bf16[448,512]{1,0:T(8,128)(2,1)S(1)}, bf16[448,512]{1,0:T(8,128)(2,1)S(1)}, u32[]{:S(2)}, u32[]{:S(2)}) collective-permute-start(bf16[448,512]{1,0:T(8,128)(2,1)S(1)} %bitcast.28), channel_id=1, source_target_pairs={{0,4},{4,0},{8,12},{12,8},{1,5},{5,1},{9,13},{13,9},{2,6},{6,2},{1... | collective-permute-start | bytes 1376264 | tf_op jit(solution)/shard_map/ppermute | solution.py:217
  15.4 2.1 %collective-permute-start.4 = (bf16[192,512]{1,0:T(8,128)(2,1)S(1)}, bf16[192,512]{1,0:T(8,128)(2,1)S(1)}, u32[]{:S(2)}, u32[]{:S(2)}) collective-permute-start(bf16[192,512]{1,0:T(8,128)(2,1)S(1)} %get-tuple-element.34), channel_id=1, source_target_pairs={{4,8},{8,4},{5,9},{9,5},{6,10},{10,6},{7,11},{11,7},{20,24},{24,20... | collective-permute-start | bytes 589832 | tf_op jit(solution)/shard_map/ppermute | solution.py:217
  16.0 10.5 %collective-permute-start.5 = (bf16[192,512]{1,0:T(8,128)(2,1)S(1)}, bf16[192,512]{1,0:T(8,128)(2,1)S(1)}, u32[]{:S(2)}, u32[]{:S(2)}) collective-permute-start(bf16[192,512]{1,0:T(8,128)(2,1)S(1)} %get-tuple-element.33), channel_id=1, source_target_pairs={{4,12},{8,0},{5,13},{9,1},{6,14},{10,2},{7,15},{11,3},{20,28},{24,... | collective-permute-start | bytes 589832 | tf_op jit(solution)/shard_map/ppermute | solution.py:217
  17.4 28.9 %copy-start.5 = (bf16[2,16,2,128]{3,2,1,0:T(2,128)(2,1)S(1)}, bf16[2,16,2,128]{3,2,1,0:T(2,128)(2,1)}, u32[]{:S(2)}) copy-start(bf16[2,16,2,128]{3,2,1,0:T(2,128)(2,1)} %param.17) | copy-start | bytes 49156
  17.4 11.8 %copy-start.6 = (bf16[192,512]{1,0:T(8,128)(2,1)}, bf16[192,512]{1,0:T(8,128)(2,1)S(1)}, u32[]{:S(2)}) copy-start(bf16[192,512]{1,0:T(8,128)(2,1)S(1)} %collective-permute-done.4.refs_9_) | copy-start | bytes 589828
  26.5 2.7 %copy-start.7 = (bf16[192,512]{1,0:T(8,128)(2,1)}, bf16[192,512]{1,0:T(8,128)(2,1)S(1)}, u32[]{:S(2)}) copy-start(bf16[192,512]{1,0:T(8,128)(2,1)S(1)} %collective-permute-done.5.refs_10_) | copy-start | bytes 589828
  28.2 14.9 %copy-start.3 = (bf16[448,512]{1,0:T(8,128)(2,1)}, bf16[448,512]{1,0:T(8,128)(2,1)S(1)}, u32[]{:S(2)}) copy-start(bf16[448,512]{1,0:T(8,128)(2,1)S(1)} %collective-permute-done.3.refs_12_) | copy-start | bytes 1376260
  29.2 9.7 %collective-permute-start.10 = (bf16[384,512]{1,0:T(8,128)(2,1)S(1)}, bf16[384,512]{1,0:T(8,128)(2,1)S(1)}, u32[]{:S(2)}, u32[]{:S(2)}) collective-permute-start(bf16[384,512]{1,0:T(8,128)(2,1)S(1)} %bitcast.23), channel_id=1, source_target_pairs={{0,4},{4,0},{8,12},{12,8},{1,5},{5,1},{9,13},{13,9},{2,6},{6,2},{1... | collective-permute-start | bytes 1179656 | tf_op jit(solution)/shard_map/ppermute | solution.py:217
  29.3 12.4 %collective-permute-start.6 = (bf16[448,512]{1,0:T(8,128)(2,1)}, bf16[448,512]{1,0:T(8,128)(2,1)}, u32[]{:S(2)}, u32[]{:S(2)}) collective-permute-start(bf16[448,512]{1,0:T(8,128)(2,1)} %get-tuple-element.30), channel_id=1, source_target_pairs={{4,8},{8,4},{5,9},{9,5},{6,10},{10,6},{7,11},{11,7},{20,24},{24,20... | collective-permute-start | bytes 1376264 | tf_op jit(solution)/shard_map/ppermute | solution.py:217
  31.4 24.8 %collective-permute-start.9 = (bf16[448,512]{1,0:T(8,128)(2,1)}, bf16[448,512]{1,0:T(8,128)(2,1)}, u32[]{:S(2)}, u32[]{:S(2)}) collective-permute-start(bf16[448,512]{1,0:T(8,128)(2,1)} %get-tuple-element.29), channel_id=1, source_target_pairs={{4,12},{8,0},{5,13},{9,1},{6,14},{10,2},{7,15},{11,3},{20,28},{24,... | collective-permute-start | bytes 1376264 | tf_op jit(solution)/shard_map/ppermute | solution.py:217
  39.8 27.3 %collective-permute-start.11 = (bf16[384,512]{1,0:T(8,128)(2,1)}, bf16[384,512]{1,0:T(8,128)(2,1)S(1)}, u32[]{:S(2)}, u32[]{:S(2)}) collective-permute-start(bf16[384,512]{1,0:T(8,128)(2,1)} %get-tuple-element.32), channel_id=1, source_target_pairs={{4,8},{8,4},{5,9},{9,5},{6,10},{10,6},{7,11},{11,7},{20,24},{24,20... | collective-permute-start | bytes 1179656 | tf_op jit(solution)/shard_map/ppermute | solution.py:217
  40.5 27.0 %collective-permute-start.12 = (bf16[384,512]{1,0:T(8,128)(2,1)S(1)}, bf16[384,512]{1,0:T(8,128)(2,1)S(1)}, u32[]{:S(2)}, u32[]{:S(2)}) collective-permute-start(bf16[384,512]{1,0:T(8,128)(2,1)S(1)} %get-tuple-element.31), channel_id=1, source_target_pairs={{4,12},{8,0},{5,13},{9,1},{6,14},{10,2},{7,15},{11,3},{20,28},{24,... | collective-permute-start | bytes 1179656 | tf_op jit(solution)/shard_map/ppermute | solution.py:217
  43.1 1.3 %collective-permute-start.7 = (f32[32,256]{1,0:T(8,128)S(1)}, f32[32,256]{1,0:T(8,128)S(1)}, u32[]{:S(2)}, u32[]{:S(2)}) collective-permute-start(f32[32,256]{1,0:T(8,128)S(1)} %fusion), channel_id=1, source_target_pairs={{0,1},{1,0},{2,3},{3,2},{4,5},{5,4},{6,7},{7,6},{8,9},{9,8},{10,11... | collective-permute-start | bytes 98312 | tf_op jit(solution)/shard_map/ppermute | solution.py:24
  44.4 4.2 %collective-permute-start.8 = (f32[32,256]{1,0:T(8,128)S(1)}, f32[32,256]{1,0:T(8,128)S(1)}, u32[]{:S(2)}, u32[]{:S(2)}) collective-permute-start(f32[32,256]{1,0:T(8,128)S(1)} %add.15), channel_id=1, source_target_pairs={{0,2},{1,3},{2,0},{3,1},{4,6},{5,7},{6,4},{7,5},{8,10},{9,11},{10,... | collective-permute-start | bytes 98312 | tf_op jit(solution)/shard_map/ppermute | solution.py:24
